TPU v7x, 32 devices: a whole 2x2x4 slice. The times are simulated.
32 devices in a mesh: batch: 2 (over x), blk: 16 (over z, y, core).
Axes of the slice: x: 2, y: 2, z: 4, core: 2. Of those that a mesh axis runs over, the one named last changes fastest.
Arguments:
- layer_input: bfloat16 [2, 4, 1024, 768], P('batch', None, 'blk'), may hold values from -6 to 6
- cotangent: bfloat16 [2, 4, 1024, 768], P('batch', None, 'blk'), may hold values from -6 to 6
- doc_lengths: int32 [2, 4, 8], P('batch'), may hold values from 0 to 1024, as said below
- joined_weight: bfloat16 [768, 2304], replicated, may hold values from -0.21875 to 0.21875
- merge_weight: bfloat16 [768, 768], replicated, may hold values from -0.21875 to 0.21875
- expand_weight: bfloat16 [768, 3072], replicated, may hold values from -0.21875 to 0.21875
- shrink_weight: bfloat16 [3072, 768], replicated, may hold values from -0.109375 to 0.109375
- first_gain: float32 [768], replicated, may hold values from 0.1 to 1.9
- mixed_gain: float32 [768], replicated, may hold values from 0.1 to 1.9
- second_gain: float32 [768], replicated, may hold values from 0.1 to 1.9
- hidden_gain: float32 [3072], replicated, may hold values from 0.1 to 1.9
Outputs:
- layer_result: bfloat16 [2, 4, 1024, 768], P('batch', None, 'blk')
- input_grad: bfloat16 [2, 4, 1024, 768], P('batch', None, 'blk')
- joined_grad: float32 [768, 2304], P('blk')
- merge_grad: float32 [768, 768], P('blk')
- expand_grad: float32 [768, 3072], P('blk')
- shrink_grad: float32 [3072, 768], P('blk')
- first_grad: float32 [768], replicated
- mixed_grad: float32 [768], replicated
- second_grad: float32 [768], replicated
- hidden_grad: float32 [3072], replicated
Inputs may be any that keep to these rules, and one draw needn't show every extreme that they name: `doc_lengths`: each stream's lengths sum to at most 1024; tokens after that sum are padding. In every group one stream holds a single document of 1024 tokens.
All inputs are finite; a program needn't handle non-finite values.
Results may differ from a plain program's by a relative error of at most 0.02.
Values may be sent and summed in bfloat16 or wider, within the bound.
No kernel may reach another device: no remote copies, remote signals or barrier semaphores. Data moves between devices by JAX's collectives and lax.ppermute only.
A program may use at most 192 MiB of HBM per device.

v0:
```python
import functools

import jax
import jax.numpy as jnp
from jax import lax
from jax.experimental import pallas as pl
from jax.experimental.pallas import tpu as pltpu
from jax.sharding import PartitionSpec as P

HEAD = 64
TILE = 256
WIDE = 512
BAND = 384
FORWARD_MIB = 14
BACKWARD_MIB = 14
WIDEN_MIB = 11
TURN_MIB = 11
OUTER_MIB = 16
big_negative = -1e30
norm_epsilon = 1e-05

f32 = jnp.float32
bf16 = jnp.bfloat16


def dot(left, right):
    return jnp.dot(left, right, preferred_element_type=f32)


def dot_nt(left, right):
    return lax.dot_general(left, right, (((1,), (1,)), ((), ())), preferred_element_type=f32)


def dot_tn(left, right):
    return lax.dot_general(left, right, (((0,), (0,)), ((), ())), preferred_element_type=f32)


def normalized(values):
    centred = values - jnp.mean(values, axis=-1, keepdims=True)
    rate = lax.rsqrt(jnp.mean(centred * centred, axis=-1, keepdims=True) + norm_epsilon)
    return centred * rate, rate


def norm_back(normal, rate, weighted):
    return rate * (
        weighted
        - jnp.mean(weighted, axis=-1, keepdims=True)
        - normal * jnp.mean(weighted * normal, axis=-1, keepdims=True)
    )


def vmem_spec():
    return pl.BlockSpec(memory_space=pltpu.VMEM)


def hbm_spec():
    return pl.BlockSpec(memory_space=pltpu.HBM)


def params(mebibytes):
    return pltpu.CompilerParams(vmem_limit_bytes=mebibytes * 1024 * 1024)


def cost(flops, moved):
    return pl.CostEstimate(flops=flops, bytes_accessed=moved, transcendentals=0)


def document_ends(lengths_ref, plane):
    ends, end = [], jnp.int32(0)
    for d in range(lengths_ref.shape[1]):
        end = end + lengths_ref[plane, d]
        ends.append(end)
    return ends


def columns_at(step):
    return pl.ds(pl.multiple_of(step * WIDE, WIDE), WIDE)


def codes(steps):
    listed = [((), 0)]
    for bit in steps:
        listed = [(at + (b,), code | (b << bit)) for at, code in listed for b in (0, 1)]
    return listed


def forward_kernel(*refs, planes, slots, seg, heads):
    place_ref, lengths_ref, gain_ref, weight_ref = refs[:4]
    pieces = refs[4 : 4 + slots * planes]
    refs = refs[4 + slots * planes :]
    length = planes * slots * seg
    tiles = length // TILE
    first_ref, joined_ref, factor_ref = refs[:3]
    sent = refs[3 : 3 + slots]
    shares = refs[3 + slots : 3 + slots + tiles]
    rows_ref, attention_ref = refs[3 + slots + tiles :]
    plane, slot = place_ref[0], place_ref[1]
    for u in range(slots):
        for k in range(planes):
            offset = ((plane ^ k) * slots + (slot ^ u)) * seg
            rows_ref[pl.ds(pl.multiple_of(offset, seg), seg), :] = pieces[k * slots + u][...]
    width = heads * HEAD

    def project(tile, carry):
        rows = pl.ds(pl.multiple_of(tile * TILE, TILE), TILE)
        normal, _ = normalized(rows_ref[rows, :].astype(f32))
        first = (normal * gain_ref[...]).astype(bf16)
        first_ref[rows, :] = first
        joined = dot(first, weight_ref[...]).astype(bf16)
        for part in range(3):
            for h in range(heads):
                column = part * width + h * HEAD
                value = joined[:, column : column + HEAD]
                if part == 0:
                    value = value * jnp.asarray(0.125, bf16)
                joined_ref[part * heads + h, rows, :] = value
        return carry

    lax.fori_loop(0, tiles, project, 0, unroll=True)
    ends = document_ends(lengths_ref, plane)
    for q in reversed(range(tiles)):
        rows = slice(q * TILE, (q + 1) * TILE)
        reach = (q + 1) * TILE
        places = q * TILE + lax.broadcasted_iota(jnp.int32, (TILE, 1), 0)
        start = jnp.zeros((TILE, 1), jnp.int32)
        for end in ends:
            start = jnp.maximum(start, jnp.where(places >= end, end, 0))
        query_pos = q * TILE + lax.broadcasted_iota(jnp.int32, (TILE, reach), 0)
        key_pos = lax.broadcasted_iota(jnp.int32, (TILE, reach), 1)
        allowed = (key_pos <= query_pos) & (key_pos >= start)
        for h in range(heads):
            scores = dot_nt(joined_ref[h, rows, :], joined_ref[heads + h, :reach, :])
            scores = jnp.where(allowed, scores, big_negative)
            peak = jnp.max(scores, axis=-1, keepdims=True)
            raised = jnp.exp(scores - peak)
            total = jnp.sum(raised, axis=-1, keepdims=True)
            share = raised.astype(bf16)
            shares[q][h] = share
            factor = 1.0 / total
            factor_ref[rows, h : h + 1] = factor
            attention_ref[h, rows, :] = factor * dot(
                share, joined_ref[2 * heads + h, :reach, :]
            )
    half = planes // 2
    for u in range(slots):
        for k in range(planes):
            offset = ((plane ^ k) * slots + (slot ^ u)) * seg
            rows = slice(k % half * seg, (k % half + 1) * seg)
            for h in range(heads):
                part = attention_ref[h, pl.ds(pl.multiple_of(offset, seg), seg), :]
                column = k // half * width + h * HEAD
                sent[u][rows, column : column + HEAD] = part.astype(bf16)


def forward_call(place, lengths, gain, weight, pieces):
    planes, slots = len(pieces), len(pieces[0])
    seg, width = pieces[0][0].shape
    length = planes * slots * seg
    heads = weight.shape[1] // (3 * HEAD)
    kernel = functools.partial(forward_kernel, planes=planes, slots=slots, seg=seg, heads=heads)
    packed = jax.ShapeDtypeStruct((planes * seg // 2, 2 * heads * HEAD), bf16)
    tiled = [(heads, TILE, reach) for reach in range(TILE, length + 1, TILE)]
    outs = pl.pallas_call(
        kernel,
        out_shape=(
            pltpu.VMEM((length, width), bf16),
            pltpu.VMEM((3 * heads, length, HEAD), bf16),
            pltpu.VMEM((length, heads), f32),
        )
        + (packed,) * slots
        + tuple(pltpu.VMEM(shape, bf16) for shape in tiled),
        in_specs=[pl.BlockSpec(memory_space=pltpu.SMEM)] * 2
        + [vmem_spec()] * (2 + slots * planes),
        out_specs=(vmem_spec(),) * (3 + slots + len(tiled)),
        scratch_shapes=[
            pltpu.VMEM((length, width), bf16),
            pltpu.VMEM((heads, length, HEAD), f32),
        ],
        compiler_params=params(FORWARD_MIB * length // 1024),
        cost_estimate=cost(8 << 30, 8 << 20),
        name="attention_forward",
    )(place, lengths, gain, weight, *[block for blocks in pieces for block in blocks])
    return outs[:3], outs[3 : 3 + slots], outs[3 + slots :]


def backward_kernel(*refs, planes, slots, seg, heads, rows_each):
    place_ref, first_ref, joined_ref, factor_ref, weight_ref, gain_ref, parts_ref = refs[:7]
    pieces = refs[7 : 7 + slots]
    length = planes * slots * seg
    tiles = length // TILE
    refs = refs[7 + slots :]
    shares = refs[:tiles]
    joined_keep, joined_give, branch_keep, branch_give = refs[tiles : tiles + 4]
    grad_ref, arrived_ref, key_ref, value_ref, total_ref, outer_ref, row_ref = refs[tiles + 4 :]
    plane, slot = place_ref[0], place_ref[1]
    width = heads * HEAD
    half = planes // 2
    for u in range(slots):
        for k in range(planes):
            offset = ((plane ^ k) * slots + (slot ^ u)) * seg
            column = k // half * width
            arrived_ref[pl.ds(pl.multiple_of(offset, seg), seg), :] = pieces[u][
                k % half * seg : (k % half + 1) * seg, column : column + width
            ]
    for h in range(heads):
        for q in reversed(range(tiles)):
            rows = slice(q * TILE, (q + 1) * TILE)
            reach = (q + 1) * TILE
            factor = factor_ref[rows, h : h + 1]
            grad = (arrived_ref[rows, h * HEAD : (h + 1) * HEAD].astype(f32) * factor).astype(bf16)
            share = shares[q][h]
            product = share.astype(f32) * dot_nt(grad, joined_ref[2 * heads + h, :reach, :])
            inner = jnp.sum(product, axis=-1, keepdims=True)
            grad_scores = (product - share.astype(f32) * (inner * factor)).astype(bf16)
            query_grad = dot(grad_scores, joined_ref[heads + h, :reach, :]) * 0.125
            grad_ref[rows, h * HEAD : (h + 1) * HEAD] = query_grad.astype(bf16)
            key_add = dot_tn(joined_ref[h, rows, :], grad_scores)
            value_add = dot_tn(grad, share)
            if q == tiles - 1:
                key_ref[...] = key_add
                value_ref[...] = value_add
            else:
                key_ref[:, :reach] += key_add
                value_ref[:, :reach] += value_add
        for part, source in ((1, key_ref), (2, value_ref)):
            column = part * width + h * HEAD
            for q in range(tiles):
                rows = slice(q * TILE, (q + 1) * TILE)
                grad_ref[rows, column : column + HEAD] = source[:, rows].T.astype(bf16)

    def back(tile, carry):
        rows = pl.ds(pl.multiple_of(tile * TILE, TILE), TILE)
        total_ref[rows, :] = dot_nt(grad_ref[rows, :], weight_ref[...])
        return carry

    lax.fori_loop(0, tiles, back, 0, unroll=True)
    for at, code in codes(range(1, bits_of(slots))):
        for out, u in ((branch_keep, code), (branch_give, code | 1)):
            for k in range(planes):
                offset = ((plane ^ k) * slots + (slot ^ u)) * seg
                out[at + (slice(k * seg, (k + 1) * seg),)] = total_ref[
                    pl.ds(pl.multiple_of(offset, seg), seg), :
                ].astype(bf16)
    model = first_ref.shape[1]
    for d in range(0, model, TILE):
        outer = dot_tn(first_ref[:, d : d + TILE], grad_ref[...])
        outer_ref[d : d + TILE, :] = outer
        scaled = jnp.sum(outer * weight_ref[d : d + TILE, :].astype(f32), axis=-1, keepdims=True)
        scaled = jnp.broadcast_to(scaled, (TILE, 128)).T
        row_ref[:, d : d + TILE] = scaled[:1] / gain_ref[:, d : d + TILE]
    wide = 3 * width
    row_ref[:, model : model + parts_ref.shape[1]] = parts_ref[...]
    gains = model + parts_ref.shape[1]
    half = planes * slots // 2
    at = 0
    for _, code in codes(range(bits_of(planes))):
        for u in range(slots):
            offset = ((plane ^ code) * slots + (slot ^ u)) * rows_each
            out = joined_keep if at < half else joined_give
            out[at % half] = outer_ref[
                pl.ds(pl.multiple_of(offset, rows_each), rows_each), :
            ].astype(bf16)
            at += 1
    joined_give[half] = jnp.zeros((rows_each, wide), bf16)
    for r in range(-(-gains // wide)):
        end = min((r + 1) * wide, gains)
        joined_give[half, r : r + 1, : end - r * wide] = row_ref[:, r * wide : end].astype(bf16)


def backward_call(
    place, first, joined, factor, weight, gain, parts, pieces, shares, planes
):
    slots = len(pieces)
    tokens = pieces[0].shape[0] * 2
    heads, length = joined.shape[0] // 3, joined.shape[1]
    width = weight.shape[0]
    rows_each = width // (planes * slots)
    kernel = functools.partial(
        backward_kernel, planes=planes, slots=slots, seg=tokens // planes, heads=heads,
        rows_each=rows_each,
    )
    pairs = (2,) * (bits_of(slots) - 1)
    wide = 3 * heads * HEAD
    row = -(-(width + parts.shape[1]) // 128) * 128
    return pl.pallas_call(
        kernel,
        out_shape=(
            jax.ShapeDtypeStruct((planes * slots // 2, rows_each, wide), bf16),
            jax.ShapeDtypeStruct((planes * slots // 2 + 1, rows_each, wide), bf16),
            jax.ShapeDtypeStruct(pairs + (tokens, width), bf16),
            jax.ShapeDtypeStruct(pairs + (tokens, width), bf16),
        ),
        in_specs=[pl.BlockSpec(memory_space=pltpu.SMEM)]
        + [vmem_spec()] * (6 + slots + len(shares)),
        out_specs=(vmem_spec(),) * 4,
        scratch_shapes=[
            pltpu.VMEM((length, wide), bf16),
            pltpu.VMEM((length, heads * HEAD), bf16),
            pltpu.VMEM((HEAD, length), f32),
            pltpu.VMEM((HEAD, length), f32),
            pltpu.VMEM((length, width), f32),
            pltpu.VMEM((width, wide), f32),
            pltpu.VMEM((1, row), f32),
        ],
        compiler_params=params(BACKWARD_MIB * length // 1024),
        cost_estimate=cost(10 << 30, 10 << 20),
        name="attention_backward",
    )(place, first, joined, factor, weight, gain, parts, *pieces, *shares)


def widen_kernel(*refs, slots, planes, groups, width, spread, block):
    place_ref = refs[0]
    pieces = refs[1 : 1 + slots]
    inputs = refs[1 + slots : 1 + slots + planes]
    refs = refs[1 + slots + planes :]
    mixed_gain_ref, second_gain_ref, hidden_gain_ref, merge_ref, expand_ref = refs[:5]
    (
        mixed_ref, middle_ref, second_ref, hidden_ref, hidden_give_ref, normal_ref, slope_ref,
        held_ref, mixed_rate_ref, hidden_rate_ref,
    ) = refs[5:15]
    (gelu_ref,) = refs[15:]
    steps = spread // WIDE

    slot = place_ref[1]
    piece = width // groups
    tokens = planes * inputs[0].shape[0]
    half = tokens // 2
    for u in range(slots):
        for side in range(2):
            held_ref[slot ^ u, side * half : (side + 1) * half, :] = pieces[u][
                :, side * piece : (side + 1) * piece
            ].astype(f32)
    mean = sum(jnp.sum(held_ref[g], axis=-1, keepdims=True) for g in range(groups)) * (1.0 / width)
    square = 0.0
    for g in range(groups):
        centred = held_ref[g] - mean
        held_ref[g] = centred
        square = square + jnp.sum(centred * centred, axis=-1, keepdims=True)
    mixed_rate = lax.rsqrt(square * (1.0 / width) + norm_epsilon)
    mixed_rate_ref[...] = mixed_rate
    middle = jnp.concatenate([block[...] for block in inputs], axis=0).astype(f32)
    for g in range(groups):
        normal = held_ref[g] * mixed_rate
        held_ref[g] = normal
        mixed = (normal * mixed_gain_ref[g]).astype(bf16)
        mixed_ref[:, g * piece : (g + 1) * piece] = mixed
        middle = middle + dot(mixed, merge_ref[g * piece : (g + 1) * piece, :])
    middle_ref[...] = middle
    second_normal, _ = normalized(middle)
    second = (second_normal * second_gain_ref[...]).astype(bf16)
    second_ref[...] = second
    total = jnp.zeros((tokens, 1), f32)

    def widen(step, total):
        at = columns_at(step)
        value = dot(second, expand_ref[:, at])
        share = 0.5 * (1.0 + lax.erf(value * 0.7071067811865476))
        gelu = value * share
        gelu_ref[:, at] = gelu
        slope = share + value * (0.3989422804014327 * jnp.exp(-0.5 * value * value))
        slope_ref[:, at] = slope.astype(bf16)
        return total + jnp.sum(gelu, axis=-1, keepdims=True)

    total = lax.fori_loop(0, steps, widen, total)
    mean = total * (1.0 / spread)
    total = jnp.zeros((tokens, 1), f32)
    for step in range(steps):
        centred = gelu_ref[:, step * WIDE : (step + 1) * WIDE] - mean
        total = total + jnp.sum(centred * centred, axis=-1, keepdims=True)
    rate = lax.rsqrt(total * (1.0 / spread) + norm_epsilon)
    hidden_rate_ref[...] = rate
    core = slot % 2
    for at in range(0, spread, 2 * BAND):
        ours, theirs = [], []
        for start in range(at, at + 2 * BAND, 2 * block):
            low = slice(start, start + block)
            high = slice(start + block, start + 2 * block)
            parts = []
            for part in (low, high):
                normal = (gelu_ref[:, part] - mean) * rate
                normal_ref[:, part] = normal.astype(bf16)
                parts.append((normal * hidden_gain_ref[:, part]).astype(bf16))
            ours.append(parts[0])
            theirs.append(parts[1])
        even, odd = jnp.concatenate(ours, axis=1), jnp.concatenate(theirs, axis=1)
        half_at = slice(at // 2, at // 2 + BAND)
        hidden_ref[:, half_at] = jnp.where(core == 0, even, odd)
        hidden_give_ref[:, half_at] = jnp.where(core == 0, odd, even)


def widen_call(
    place, pieces, inputs, mixed_gain, second_gain, hidden_gain, merge, expand
):
    slots = len(pieces)
    tokens = len(inputs) * inputs[0].shape[0]
    piece = pieces[0].shape[1] // 2
    width, spread = expand.shape
    groups = width // piece

    def low(*shape):
        return jax.ShapeDtypeStruct(shape, bf16)

    def full(*shape):
        return jax.ShapeDtypeStruct(shape, f32)

    return pl.pallas_call(
        functools.partial(
            widen_kernel, slots=slots, planes=len(inputs), groups=groups, width=width,
            spread=spread, block=spread // (slots * len(inputs)),
        ),
        out_shape=(
            low(tokens, width),
            full(tokens, width),
            low(tokens, width),
            low(tokens, spread // 2),
            low(tokens, spread // 2),
            low(tokens, spread),
            low(tokens, spread),
            full(slots, tokens, piece),
            full(tokens, 1),
            full(tokens, 1),
        ),
        in_specs=[pl.BlockSpec(memory_space=pltpu.SMEM)]
        + [vmem_spec()] * (5 + slots + len(inputs)),
        out_specs=(vmem_spec(),) * 10,
        scratch_shapes=[
            pltpu.VMEM((tokens, spread), f32),
        ],
        compiler_params=params(WIDEN_MIB),
        cost_estimate=cost(6 << 30, 6 << 20),
        name="widen",
    )(
        place, *pieces, *inputs, mixed_gain, second_gain, hidden_gain, merge, expand,
    )


def branch_kernel(place_ref, lengths_ref, *refs, slots):
    blocks, branch_ref = refs[:-1], refs[-1]
    seg = blocks[0].shape[0]
    limit = document_ends(lengths_ref, place_ref[0])[-1]
    for k, block in enumerate(blocks):
        offset = ((place_ref[0] ^ k) * slots + place_ref[1]) * seg
        valid = offset + lax.broadcasted_iota(jnp.int32, (seg, 1), 0) < limit
        branch_ref[k * seg : (k + 1) * seg, :] = jnp.where(
            valid, block[...], jnp.zeros((), bf16)
        )


def branch_call(place, lengths, blocks, slots):
    seg, width = blocks[0].shape
    return pl.pallas_call(
        functools.partial(branch_kernel, slots=slots),
        out_shape=jax.ShapeDtypeStruct((len(blocks) * seg, width), bf16),
        in_specs=[pl.BlockSpec(memory_space=pltpu.SMEM)] * 2 + [vmem_spec()] * len(blocks),
        out_specs=vmem_spec(),
        compiler_params=params(4),
        name="branch",
    )(place, lengths, *blocks)


def turn_kernel(*refs, slots, planes, groups, width, spread):
    (
        place_ref, branch_ref, normal_ref, slope_ref, middle_ref, held_ref,
        mixed_rate_ref, hidden_rate_ref,
        mixed_gain_ref, second_gain_ref, hidden_gain_ref, merge_ref, shrink_ref, expand_ref,
    ) = refs[:14]
    expanded_ref, mix_ref, grad_ref, parts_ref = refs[14:18]
    away = refs[18 : 18 + slots]
    results = refs[18 + slots : 18 + slots + planes]
    weighted_ref, sent_ref = refs[18 + slots + planes :]
    steps = spread // WIDE

    slot = place_ref[1]
    piece = width // groups
    tokens = middle_ref.shape[0]
    half = tokens // 2
    branch = branch_ref[...]
    result = middle_ref[...]
    weighted_sum = jnp.zeros((tokens, 1), f32)
    inner_sum = jnp.zeros((tokens, 1), f32)
    for step in range(steps):
        at = slice(step * WIDE, (step + 1) * WIDE)
        normal = normal_ref[:, at].astype(f32)
        hidden = (normal * hidden_gain_ref[:, at]).astype(bf16)
        result = result + dot(hidden, shrink_ref[at, :])
        grad_hidden = dot_nt(branch, shrink_ref[at, :])
        start = 2 * width + step * WIDE
        parts_ref[:, start : start + WIDE] = jnp.sum(grad_hidden * normal, axis=0, keepdims=True)
        weighted = grad_hidden * hidden_gain_ref[:, at]
        weighted_ref[:, at] = weighted
        weighted_sum = weighted_sum + jnp.sum(weighted, axis=-1, keepdims=True)
        inner_sum = inner_sum + jnp.sum(weighted * normal, axis=-1, keepdims=True)
    seg = tokens // planes
    for k in range(planes):
        results[k][...] = result[k * seg : (k + 1) * seg, :].astype(bf16)
    weighted_mean = weighted_sum * (1.0 / spread)
    inner_mean = inner_sum * (1.0 / spread)
    rate = hidden_rate_ref[...]
    grad_second = jnp.zeros((tokens, width), f32)
    for step in range(steps):
        at = slice(step * WIDE, (step + 1) * WIDE)
        grad = rate * (
            weighted_ref[:, at] - weighted_mean - normal_ref[:, at].astype(f32) * inner_mean
        )
        expanded = (grad * slope_ref[:, at].astype(f32)).astype(bf16)
        expanded_ref[:, at] = expanded
        grad_second = grad_second + dot_nt(expanded, expand_ref[:, at])
    second_normal, second_rate = normalized(middle_ref[...])
    parts_ref[:, width : 2 * width] = jnp.sum(grad_second * second_normal, axis=0, keepdims=True)
    grad_middle = branch.astype(f32) + norm_back(
        second_normal, second_rate, grad_second * second_gain_ref[...]
    )
    grad_ref[...] = grad_middle
    mix = grad_middle.astype(bf16)
    mix_ref[...] = mix
    grads = []
    weighted_sum = 0.0
    inner_sum = 0.0
    for g in range(groups):
        grad_mixed = dot_nt(mix, merge_ref[g * piece : (g + 1) * piece, :])
        parts_ref[:, g * piece : (g + 1) * piece] = jnp.sum(
            grad_mixed * held_ref[g], axis=0, keepdims=True
        )
        weighted = grad_mixed * mixed_gain_ref[g]
        grads.append(weighted)
        weighted_sum = weighted_sum + jnp.sum(weighted, axis=-1, keepdims=True)
        inner_sum = inner_sum + jnp.sum(weighted * held_ref[g], axis=-1, keepdims=True)
    weighted_mean = weighted_sum * (1.0 / width)
    inner_mean = inner_sum * (1.0 / width)
    for g in range(slots):
        if g < groups:
            sent_ref[g] = mixed_rate_ref[...] * (
                grads[g] - weighted_mean - held_ref[g] * inner_mean
            )
        else:
            sent_ref[g] = jnp.zeros(sent_ref.shape[1:], f32)
    for u in range(slots):
        for side in range(2):
            away[u][:, side * piece : (side + 1) * piece] = sent_ref[
                slot ^ u, side * half : (side + 1) * half, :
            ].astype(bf16)


def turn_call(
    place, branch, normal, slope, middle, held, mixed_rate, hidden_rate,
    mixed_gain, second_gain, hidden_gain, merge, shrink, expand, planes,
):
    slots, tokens, piece = held.shape
    width, spread = expand.shape
    groups = width // piece

    def low(*shape):
        return jax.ShapeDtypeStruct(shape, bf16)

    def full(*shape):
        return jax.ShapeDtypeStruct(shape, f32)

    outs = pl.pallas_call(
        functools.partial(
            turn_kernel, slots=slots, planes=planes, groups=groups, width=width, spread=spread
        ),
        out_shape=(
            low(tokens, spread),
            low(tokens, width),
            full(tokens, width),
            full(1, 2 * width + spread),
        )
        + (low(tokens // 2, 2 * piece),) * slots
        + (low(tokens // planes, width),) * planes,
        in_specs=[pl.BlockSpec(memory_space=pltpu.SMEM)] + [vmem_spec()] * 13,
        out_specs=(vmem_spec(),) * (4 + slots + planes),
        scratch_shapes=[
            pltpu.VMEM((tokens, spread), f32),
            pltpu.VMEM((slots, tokens, piece), f32),
        ],
        compiler_params=params(TURN_MIB),
        cost_estimate=cost(9 << 30, 8 << 20),
        name="turn",
    )(
        place, branch, normal, slope, middle, held, mixed_rate, hidden_rate,
        mixed_gain, second_gain, hidden_gain, merge, shrink, expand,
    )
    return outs[:4], outs[4 : 4 + slots], outs[4 + slots :]


def cut_out(outs, total_ref, place_ref, bands, steps, rows_each, axis, cut):
    whole_ref, firsts = outs[0], outs[1:]
    far_rank, side = place_ref[2] // 2, place_ref[3]
    for at, code in codes(steps):
        other, far = code & 1, code >> 1
        offset = pl.multiple_of((far_rank ^ far) * rows_each, rows_each)
        parts = []
        for first, wide in bands:
            column = pl.multiple_of(first + (side ^ other) * wide, 128)
            parts.append(
                total_ref[pl.ds(offset, rows_each), pl.ds(column, wide)].astype(bf16)
            )
        value = parts[0] if len(parts) == 1 else jnp.concatenate(parts, axis=1)
        whole_ref[at] = value
        for chain, first_ref in enumerate(firsts):
            if at[chain] == 1:
                band = slice(0, cut) if chain == 0 else slice(cut, None)
                first_ref[at[:chain] + at[chain + 1 :]] = (
                    value[band] if axis == 0 else value[:, band]
                )


def shrink_kernel(
    place_ref, hidden_ref, branch_ref, hidden_got_ref, branch_got_ref, *refs, cutting
):
    total_ref = refs[-1]
    spread, _ = total_ref.shape
    branch = jnp.concatenate([branch_ref[...], branch_got_ref[...]], axis=0)

    def multiply(step, carry):
        at = columns_at(step)
        hidden = jnp.concatenate([hidden_ref[:, at], hidden_got_ref[:, at]], axis=0)
        total_ref[at, :] = dot_tn(hidden, branch)
        return carry

    lax.fori_loop(0, spread // WIDE, multiply, 0)
    cut_out(refs[:-1], total_ref, place_ref, **cutting)


def expand_kernel(
    place_ref, second_ref, mixed_ref, second_got_ref, mixed_got_ref,
    expanded_ref, mix_ref, expanded_got_ref, mix_got_ref, *refs, cutting,
):
    turned_ref, total_ref = refs[-2:]
    tokens, spread = expanded_ref.shape
    width = second_ref.shape[1]
    core = place_ref[2] % 2
    rows_each = cutting["rows_each"]

    def left(own_ref, got_ref):
        turned_ref[:, :tokens] = own_ref[...].astype(f32).T
        turned_ref[:, tokens:] = got_ref[...].astype(f32).T
        rows = [
            turned_ref[pl.ds(pl.multiple_of((2 * i + core) * rows_each, rows_each), rows_each), :]
            for i in range(width // (2 * rows_each))
        ]
        return jnp.concatenate(rows, axis=0).astype(bf16)

    second = left(second_ref, second_got_ref)
    for at in range(0, spread, WIDE):
        band = slice(at, at + WIDE)
        total_ref[:, band] = dot(
            second, jnp.concatenate([expanded_ref[:, band], expanded_got_ref[:, band]], axis=0)
        )
    mixed = left(mixed_ref, mixed_got_ref)
    total_ref[:, spread:] = dot(
        mixed, jnp.concatenate([mix_ref[...], mix_got_ref[...]], axis=0)
    )
    cut_out(refs[:-2], total_ref, place_ref, **cutting)


def outer_call(kernel, place, operands, rows, columns, bands, steps, size, axis, cut, scratch, name):
    rows_each = rows // size
    shape = (rows_each, columns // 2)
    low = (cut, shape[1]) if axis == 0 else (shape[0], cut)
    high = (shape[0] - cut, shape[1]) if axis == 0 else (shape[0], shape[1] - cut)
    pairs = (2,) * (len(steps) - 1)
    return pl.pallas_call(
        functools.partial(
            kernel,
            cutting=dict(bands=bands, steps=steps, rows_each=rows_each, axis=axis, cut=cut),
        ),
        out_shape=(
            jax.ShapeDtypeStruct((2,) + pairs + shape, bf16),
            jax.ShapeDtypeStruct(pairs + low, bf16),
            jax.ShapeDtypeStruct(pairs + high, bf16),
        ),
        in_specs=[pl.BlockSpec(memory_space=pltpu.SMEM)] + [vmem_spec()] * len(operands),
        out_specs=(vmem_spec(),) * 3,
        scratch_shapes=scratch + [pltpu.VMEM((rows // 2, columns), f32)],
        compiler_params=params(OUTER_MIB),
        cost_estimate=cost(2 << 30, 10 << 20),
        name=name,
    )(place, *operands)


def settle_kernel(place_ref, *refs):
    out = refs[-1]
    for k, ref in enumerate(refs[:-1]):
        out[place_ref[0] ^ k] = ref[...]


def settle_call(place, blocks):
    return pl.pallas_call(
        settle_kernel,
        out_shape=jax.ShapeDtypeStruct((len(blocks),) + blocks[0].shape, blocks[0].dtype),
        in_specs=[pl.BlockSpec(memory_space=pltpu.SMEM)] + [vmem_spec()] * len(blocks),
        out_specs=vmem_spec(),
        compiler_params=params(8),
        name="settle",
    )(place, *blocks)


def joined_slots_kernel(*refs, held):
    sources, outs = refs[:held], refs[held:]
    last = len(outs)
    for u, out in enumerate(outs):
        out[0] = sum(ref[u].astype(f32) for ref in sources).astype(bf16)
        out[1] = sum(ref[last].astype(f32) for ref in sources).astype(bf16)


def joined_slots_call(held, slots):
    _, rows, wide = held[0].shape
    return pl.pallas_call(
        functools.partial(joined_slots_kernel, held=len(held)),
        out_shape=(jax.ShapeDtypeStruct((2, rows, wide), bf16),) * slots,
        in_specs=[vmem_spec()] * len(held),
        out_specs=(vmem_spec(),) * slots,
        compiler_params=params(4),
        name="joined_slots",
    )(*held)


def heads_kernel(place_ref, *refs, groups, gains):
    joined_out, gains_out, held_ref = refs[-3:]
    pieces = refs[:-3]
    sums = []
    for u, ref in enumerate(pieces):
        held_ref[place_ref[1] ^ u] = ref[0].astype(f32)
        sums.append(ref[1].astype(f32))
    piece = pieces[0].shape[2] // 3
    for part in range(3):
        for g in range(groups):
            start = (part * groups + g) * piece
            joined_out[:, start : start + piece] = held_ref[
                g, :, part * piece : (part + 1) * piece
            ]
    while len(sums) > 1:
        sums = [sums[i] + sums[i + 1] for i in range(0, len(sums), 2)]
    wide = 3 * piece
    for r in range(-(-gains // wide)):
        end = min((r + 1) * wide, gains)
        gains_out[:, r * wide : end] = sums[0][r : r + 1, : end - r * wide]


def heads_call(place, blocks, width, gains):
    _, rows, wide = blocks[0].shape
    return pl.pallas_call(
        functools.partial(heads_kernel, groups=3 * width // wide, gains=gains),
        out_shape=(
            jax.ShapeDtypeStruct((rows, 3 * width), f32),
            jax.ShapeDtypeStruct((1, gains), f32),
        ),
        in_specs=[pl.BlockSpec(memory_space=pltpu.SMEM)] + [vmem_spec()] * len(blocks),
        out_specs=(vmem_spec(),) * 2,
        scratch_shapes=[pltpu.VMEM((len(blocks), rows, wide), f32)],
        compiler_params=params(8),
        name="heads_side_by_side",
    )(place, *blocks)


def input_kernel(*refs, planes, parts):
    inputs = refs[:planes]
    refs = refs[planes:]
    grad_ref, gain_ref = refs[:2]
    grad = sum(ref[at].astype(f32) for ref, at in zip(refs[2 : 2 + len(parts)], parts))
    outs = refs[2 + len(parts) :]
    normal, rate = normalized(
        jnp.concatenate([block[...] for block in inputs], axis=0).astype(f32)
    )
    value = grad_ref[...] + norm_back(normal, rate, grad * gain_ref[...])
    seg = value.shape[0] // planes
    for k in range(planes):
        outs[k][...] = value[k * seg : (k + 1) * seg, :].astype(bf16)


def input_call(inputs, grad_middle, gain, held, parts):
    planes = len(inputs)
    tokens, width = grad_middle.shape
    return pl.pallas_call(
        functools.partial(input_kernel, planes=planes, parts=parts),
        out_shape=(jax.ShapeDtypeStruct((tokens // planes, width), bf16),) * planes,
        in_specs=[vmem_spec()] * (2 + planes + len(held)),
        out_specs=(vmem_spec(),) * planes,
        compiler_params=params(16),
        name="input_back",
    )(*inputs, grad_middle, gain, *held)


def swap(value, axis, bits):
    size = lax.axis_size(axis)
    return lax.ppermute(value, axis, [(i, i ^ bits) for i in range(size)])


def pick(value, index, axis=0):
    return lax.dynamic_index_in_dim(value, index, axis, keepdims=False)


def in_hbm(*values):
    return [pltpu.with_memory_space_constraint(value, pltpu.HBM) for value in values]


def bits_of(size):
    return size.bit_length() - 1


def sums_kernel(*refs, listed, together):
    outs = refs[-1:] if together else refs[-len(listed) :]
    start = 0
    for i, terms in enumerate(listed):
        value = sum(refs[j][at].astype(f32) for j, at in terms).astype(bf16)
        if together:
            end = start + value.shape[together]
            outs[0][(..., slice(start, end)) + (slice(None),) * (-1 - together)] = value
            start = end
        else:
            outs[i][...] = value


def sums_call(sums, name, together=0):
    arrays, listed, shapes = [], [], []
    for terms in sums:
        entry = []
        for array, at in terms:
            where = [i for i, held in enumerate(arrays) if held is array]
            if not where:
                arrays.append(array)
                where = [len(arrays) - 1]
            entry.append((where[0], at))
        listed.append(entry)
        shapes.append(jax.eval_shape(lambda v, at=terms[0][1]: v[at], terms[0][0]).shape)
    if together:
        shape = list(shapes[0])
        shape[together] = sum(shape[together] for shape in shapes)
        shapes = [tuple(shape)]
    outs = pl.pallas_call(
        functools.partial(sums_kernel, listed=listed, together=together),
        out_shape=tuple(jax.ShapeDtypeStruct(shape, bf16) for shape in shapes),
        in_specs=[vmem_spec()] * len(arrays),
        out_specs=(vmem_spec(),) * len(shapes),
        compiler_params=params(4),
        name=name,
    )(*arrays)
    return outs[0] if together or len(shapes) == 1 else outs


class Halves:
    def __init__(self):
        self.entries = []
        self.chosen = {}

    def hold(self, array, names, bands=()):
        self.entries.append((array, names, dict(bands)))

    def terms(self, choice=()):
        chosen = dict(self.chosen)
        chosen.update(choice)
        return [
            (
                array,
                tuple(chosen[n] if n in chosen else bands.get(n, slice(None)) for n in names),
            )
            for array, names, bands in self.entries
        ]

    def receive(self, name, array, bands=()):
        self.chosen[name] = 0
        names = [n for n in self.entries[0][1] if n not in self.chosen]
        self.hold(array, names, bands)


def sides_kernel(place_ref, own_ref, other_ref, *outs):
    first = place_ref[3] == 0
    own, other = own_ref[...].astype(f32), other_ref[...].astype(f32)
    low, high = jnp.where(first, own, other), jnp.where(first, other, own)
    start = 0
    for out in outs:
        wide = out.shape[1] // 2
        out[:, :wide] = low[:, start : start + wide]
        out[:, wide:] = high[:, start : start + wide]
        start += wide


def sides_call(place, own, other, widths, name):
    rows = own.shape[0]
    return pl.pallas_call(
        sides_kernel,
        out_shape=tuple(jax.ShapeDtypeStruct((rows, wide), f32) for wide in widths),
        in_specs=[pl.BlockSpec(memory_space=pltpu.SMEM)] + [vmem_spec()] * 2,
        out_specs=(vmem_spec(),) * len(widths),
        compiler_params=params(8),
        name=name,
    )(place, own, other)


def per_device(
    layer_input, cotangent, doc_lengths, joined_weight, merge_weight, expand_weight,
    shrink_weight, first_gain, mixed_gain, second_gain, hidden_gain,
):
    _, planes, seg, width = layer_input.shape
    size = lax.axis_size("blk")
    slots = size // planes
    batches = lax.axis_size("batch")
    rank = lax.axis_index("blk")
    group_rank = lax.axis_index("batch")
    plane = rank // slots
    slot = rank % slots
    head_count = width // HEAD
    heads = -(-head_count // slots)
    groups = head_count // heads
    piece = heads * HEAD
    tokens = planes * seg
    length = slots * tokens
    side = group_rank % 2
    place = jnp.stack([plane, slot, rank, side]).astype(jnp.int32)

    def to_planes(blocks):
        return [pick(blocks, plane)] + [
            swap(pick(blocks, plane ^ k), "blk", k * slots) for k in range(1, planes)
        ]

    def all_slots(value):
        held = {0: value}
        for bit in reversed(range(bits_of(slots))):
            held.update({u | 1 << bit: swap(v, "blk", 1 << bit) for u, v in held.items()})
        return [held[u] for u in range(slots)]

    def over_slots(blocks):
        return [blocks[0]] + [swap(blocks[u], "blk", u) for u in range(1, slots)]

    spread = expand_weight.shape[1]
    first_arrived = to_planes(layer_input[0])
    own_start = jnp.minimum(slot, groups - 1) * piece
    own_weight = jnp.concatenate(
        [
            lax.dynamic_slice_in_dim(joined_weight, part * width + own_start, piece, 1)
            for part in range(3)
        ],
        axis=1,
    )
    lengths = doc_lengths[0]
    gain_row = first_gain.reshape(1, width)
    mixed_gain = mixed_gain.reshape(groups, 1, piece)
    second_gain = second_gain.reshape(1, width)
    hidden_gain = hidden_gain.reshape(1, spread)
    (
        first_arrived[-1], place, lengths, gain_row, mixed_gain, second_gain, hidden_gain, own_weight,
    ) = lax.optimization_barrier(
        (
            first_arrived[-1], place, lengths, gain_row, mixed_gain, second_gain, hidden_gain,
            own_weight,
        )
    )
    pieces = [all_slots(block) for block in first_arrived]
    (first, joined, factor), sent, shares = forward_call(
        place, lengths, gain_row, own_weight, pieces
    )
    sent, cotangent = lax.optimization_barrier((sent, cotangent))
    cotangent_blocks = to_planes(cotangent[0])
    (
        mixed, middle, second, hidden, hidden_give, normal, slope, held, mixed_rate, hidden_rate,
    ) = widen_call(
        place, over_slots(sent), first_arrived, mixed_gain, second_gain, hidden_gain, merge_weight,
        expand_weight,
    )
    hidden_give, cotangent_blocks = lax.optimization_barrier((hidden_give, cotangent_blocks))
    branch = branch_call(place, lengths, cotangent_blocks, slots)

    row_bits = list(range(1, bits_of(slots)))
    plane_bits = list(range(bits_of(slots), bits_of(size)))
    names = ["side"] + row_bits + plane_bits + ["rows", "columns"]
    steps = [0] + row_bits + plane_bits
    orders = (["side"] + row_bits, row_bits + ["side"])
    stages = len(orders[0])

    def cross(name, value):
        return swap(value, "batch", 1) if name == "side" else swap(value, "blk", 1 << name)

    def chains(axis, cut, whole):
        pair = [Halves(), Halves()]
        for chain, band in zip(pair, (slice(0, cut), slice(cut, None))):
            chain.hold(whole, names, {axis: band})
        return pair

    def sends(pair, at):
        return sums_call(
            [chain.terms({order[at]: 1}) for chain, order in zip(pair, orders)], "next_halves"
        )

    def crossed(at, values):
        return [cross(order[at], value) for order, value in zip(orders, values)]

    def arrive(pair, at, values):
        for chain, order, value in zip(pair, orders, values):
            chain.receive(order[at], value)

    def plane_depart(pair, bit, axis):
        together = -2 if axis == "rows" else -1
        return cross(
            bit, sums_call([chain.terms({bit: 1}) for chain in pair], "plane_halves", together)
        )

    def plane_arrive(pair, bit, axis, both):
        cut = pair[0].entries[0][2][axis].stop
        for chain, band in zip(pair, (slice(0, cut), slice(cut, None))):
            chain.receive(bit, both, {axis: band})

    def closed(pair, axis):
        together = -2 if axis == "rows" else -1
        value = sums_call([chain.terms() for chain in pair], "last_halves", together)
        for bit in range(1, bits_of(batches)):
            value = sums_call([[(value, ...), (swap(value, "batch", 1 << bit), ...)]], "groups")
        return value, swap(value, "batch", 1)

    cut = spread // size // 2
    shrink_whole, *shrink_firsts = outer_call(
        shrink_kernel, place,
        [hidden, branch, swap(hidden_give, "blk", 1), swap(branch, "blk", 1)],
        spread, width, ((0, width // 2),), steps, size, 0, cut, [], "shrink_outer",
    )
    shrink_sent = crossed(0, shrink_firsts)
    second_got, mixed_got = swap(second, "blk", 1), swap(mixed, "blk", 1)
    (expanded, mix, grad_middle, parts), away, results = turn_call(
        place, branch, normal, slope, middle, held, mixed_rate, hidden_rate,
        mixed_gain, second_gain, hidden_gain, merge_weight, shrink_weight, expand_weight, planes,
    )
    shrink_sent, second_got, mixed_got, expanded, mix = lax.optimization_barrier(
        (shrink_sent, second_got, mixed_got, expanded, mix)
    )
    shrink_chains = chains("rows", cut, shrink_whole)
    arrive(shrink_chains, 0, shrink_sent)

    returned = over_slots(away)
    expanded_got, mix_got = swap(expanded, "blk", 1), swap(mix, "blk", 1)
    returned, expanded_got, mix_got = lax.optimization_barrier((returned, expanded_got, mix_got))
    cut = ((spread + width) // 4 + 127) // 128 * 128
    expand_whole, *expand_firsts = outer_call(
        expand_kernel, place,
        [second, mixed, second_got, mixed_got, expanded, mix, expanded_got, mix_got],
        width, spread + width, ((0, spread // 2), (spread, width // 2)), steps, size, 1, cut,
        [pltpu.VMEM((width, 2 * tokens), f32)], "expand_outer",
    )
    for at in range(1, stages):
        shrink_sent = crossed(at, sends(shrink_chains, at))
        if at < stages - 1:
            arrive(shrink_chains, at, shrink_sent)
    expand_firsts, results = lax.optimization_barrier((expand_firsts, results))
    result_blocks = [results[0]] + [
        swap(results[k], "blk", k * slots) for k in range(1, planes)
    ]
    returned, expand_firsts, shrink_sent = lax.optimization_barrier(
        (returned, expand_firsts, shrink_sent)
    )
    arrive(shrink_chains, stages - 1, shrink_sent)
    expand_sent = crossed(0, expand_firsts)
    shrink_both = plane_depart(shrink_chains, plane_bits[0], "rows")
    joined_keep, joined_give, branch_keep, branch_give = backward_call(
        place, first, joined, factor, own_weight, gain_row, parts, returned, shares, planes
    )
    (
        joined_give, branch_give, shrink_both, expand_sent, result_blocks,
    ) = lax.optimization_barrier(
        (joined_give, branch_give, shrink_both, expand_sent, result_blocks)
    )
    plane_arrive(shrink_chains, plane_bits[0], "rows", shrink_both)
    expand_chains = chains("columns", cut, expand_whole)
    arrive(expand_chains, 0, expand_sent)

    joined_got = swap(joined_give, "blk", 1 << plane_bits[0])
    branch_got = swap(branch_give, "blk", 1)
    for at in range(1, stages):
        expand_sent = crossed(at, sends(expand_chains, at))
        if at < stages - 1:
            arrive(expand_chains, at, expand_sent)
    for bit in plane_bits[1:]:
        shrink_both = plane_depart(shrink_chains, bit, "rows")
        if bit != plane_bits[-1]:
            plane_arrive(shrink_chains, bit, "rows", shrink_both)
    branch_held, prefixes = [branch_keep, branch_got], [(), ()]
    for bit in row_bits:
        give = sums_call(
            [[(v, p + (1,)) for v, p in zip(branch_held, prefixes)]], "branch_halves"
        )
        prefixes = [p + (0,) for p in prefixes] + [()]
        branch_held.append(swap(give, "blk", 1 << bit))
    joined_got, branch_held[-1], expand_sent, shrink_both = lax.optimization_barrier(
        (joined_got, branch_held[-1], expand_sent, shrink_both)
    )
    arrive(expand_chains, stages - 1, expand_sent)
    plane_arrive(shrink_chains, plane_bits[-1], "rows", shrink_both)

    expand_both = plane_depart(expand_chains, plane_bits[0], "columns")
    joined_terms = [(joined_keep, 0), (joined_got, 0)]
    blocks = planes * slots // 2
    gain_terms = [(joined_give, blocks), (joined_got, blocks)]
    for bit in plane_bits[1:]:
        blocks //= 2
        joined_give = sums_call(
            [
                [(v, slice(start + blocks, start + 2 * blocks)) for v, start in joined_terms],
                [(v, slice(at, at + 1)) for v, at in gain_terms],
            ],
            "joined_halves", -3,
        )
        joined_got = swap(joined_give, "blk", 1 << bit)
        joined_terms.append((joined_got, 0))
        gain_terms = [(joined_give, blocks), (joined_got, blocks)]
    input_blocks = input_call(
        first_arrived, grad_middle, gain_row, branch_held, prefixes
    )
    input_blocks = [input_blocks[0]] + [
        swap(input_blocks[k], "blk", k * slots) for k in range(1, planes)
    ]
    joined_last = sums_call(
        [
            [(v, slice(start, start + slots)) for v, start in joined_terms],
            [(v, slice(at, at + 1)) for v, at in gain_terms],
        ],
        "joined_last", -3,
    )
    held = [joined_last]
    for bit in range(bits_of(batches)):
        if len(held) > 1:
            held = [sums_call([[(v, ...) for v in held]], "joined_groups")]
        held.append(swap(held[0], "batch", 1 << bit))
    joined_sent = joined_slots_call(held, slots)
    joined_grad, gain_grads = heads_call(
        place,
        [joined_sent[0]] + [swap(joined_sent[u], "blk", u) for u in range(1, slots)],
        width, 3 * width + spread,
    )
    shrink_grad, = sides_call(place, *closed(shrink_chains, "rows"), (width,), "shrink_sides")
    plane_arrive(expand_chains, plane_bits[0], "columns", expand_both)
    for bit in plane_bits[1:]:
        expand_both = plane_depart(expand_chains, bit, "columns")
        plane_arrive(expand_chains, bit, "columns", expand_both)
    expand_grad, merge_grad = sides_call(
        place, *closed(expand_chains, "columns"), (spread, width), "expand_sides"
    )
    layer_result = settle_call(place, result_blocks).reshape(layer_input.shape)
    input_grad = settle_call(place, input_blocks).reshape(layer_input.shape)
    gain_grads = gain_grads[0]
    return (
        layer_result, input_grad, joined_grad, merge_grad, expand_grad,
        shrink_grad, gain_grads[:width], gain_grads[width : 2 * width],
        gain_grads[2 * width : 3 * width], gain_grads[3 * width :],
    )


def solution(mesh):
    rows = P("batch", None, "blk", None)
    return jax.shard_map(
        per_device,
        mesh=mesh,
        in_specs=(rows, rows, P("batch", None, None)) + (P(),) * 8,
        out_specs=(rows, rows) + (P("blk", None),) * 4 + (P(),) * 4,
        check_vma=False,
    )
```

profile of v0, /device:TPU:0, one launch (start us, length us, event | category | flops | bytes accessed | tf_op | source)
XLA Modules:
  0.0 170.2 jit_solution(12151674268579968008)
XLA Ops:
  2.3 2.6 %collective-permute-start.2 = (bf16[64,768]{1,0:T(8,128)(2,1)S(1)}, bf16[64,768]{1,0:T(8,128)(2,1)S(1)}, u32[]{:S(2)}, u32[]{:S(2)}) collective-permute-start(bf16[64,768]{1,0:T(8,128)(2,1)S(1)} %get-tuple-element.255.refs_4_.refs_5_.refs_0_), channel_id=1, source_target_pairs={{0,2},{1,3},{2,0},{3,1},{4,6},{5,7},{6,4},{7,5},{8,10},{9,11},{10,... | collective-permute-start | bytes 294920 | tf_op jit(solution)/shard_map/ppermute | solution.py:787
  4.9 3.6 %collective-permute-start = (bf16[64,768]{1,0:T(8,128)(2,1)S(1)}, bf16[64,768]{1,0:T(8,128)(2,1)S(1)}, u32[]{:S(2)}, u32[]{:S(2)}) collective-permute-start(bf16[64,768]{1,0:T(8,128)(2,1)S(1)} %get-tuple-element.256), channel_id=1, source_target_pairs={{0,12},{1,13},{2,14},{3,15},{4,8},{5,9},{6,10},{7,11},{8,4},{9,5},... | collective-permute-start | bytes 294920 | tf_op jit(solution)/shard_map/ppermute | solution.py:787
  11.4 2.0 %constant_dynamic-slice_fusion.2 = (bf16[768,192]{1,0:T(8,128)(2,1)S(1)}, bf16[768,192]{1,0:T(8,128)(2,1)S(1)}, bf16[768,192]{1,0:T(8,128)(2,1)S(1)}) fusion(bf16[768,2304]{1,0:T(8,128)(2,1)} %param.14, s32[]{:T(128)S(6)} %select_n.45, s32[]{:T(128)S(6)} %select_n.47, s32[]{:T(128)S(6)} %select_n.46), kind=kLoop, calls=%fused_computation.14 | loop fusion | bytes 1769484 | tf_op jit(solution)/shard_map/dynamic_slice | solution.py:931
  20.4 2.4 %collective-permute-done.10.refs_14_ = bf16[64,768]{1,0:T(8,128)(2,1)S(1)} collective-permute-done((bf16[64,768]{1,0:T(8,128)(2,1)S(1)}, bf16[64,768]{1,0:T(8,128)(2,1)S(1)}, u32[]{:S(2)}, u32[]{:S(2)}) %collective-permute-start.10) | collective-permute-done | bytes 98336 | tf_op jit(solution)/shard_map/ppermute | solution.py:787
  25.5 7.8 %attention_forward.1 = (bf16[1024,768]{1,0:T(8,128)(2,1)S(1)}, bf16[9,1024,64]{2,1,0:T(8,128)(2,1)S(1)}, f32[1024,3]{1,0:T(8,128)S(1)}, bf16[128,384]{1,0:T(8,12...) custom-call(s32[4]{0:T(128)S(1)} %pad_add_fusion.refs_0_.place_ref, ...), custom_call_target="tpu_custom_call" | custom-call | flops 8589934592 | bytes 8388608 | tf_op jit(solution)/shard_map/attention_forward/pallas_call | solution.py:163
  36.8 1.9 %collective-permute-start.19 = (bf16[64,768]{1,0:T(8,128)(2,1)S(1)}, bf16[64,768]{1,0:T(8,128)(2,1)S(1)}, u32[]{:S(2)}, u32[]{:S(2)}) collective-permute-start(bf16[64,768]{1,0:T(8,128)(2,1)S(1)} %get-tuple-element.251), channel_id=1, source_target_pairs={{0,8},{1,9},{2,10},{3,11},{4,12},{5,13},{6,14},{7,15},{8,0},{9,1},... | collective-permute-start | bytes 294920 | tf_op jit(solution)/shard_map/ppermute | solution.py:787
  40.1 7.1 %widen.1 = (bf16[256,768]{1,0:T(8,128)(2,1)S(1)}, f32[256,768]{1,0:T(8,128)S(1)}, bf16[256,768]{1,0:T(8,128)(2,1)S(1)}, bf16[256,1536]{1,0:T(8,128)(2,1)S(1)}, b...) custom-call(s32[4]{0:T(128)S(1)} %pad_add_fusion.refs_0_.place_ref, ...), custom_call_target="tpu_custom_call" | custom-call | flops 6442450944 | bytes 6291456 | tf_op jit(solution)/shard_map/widen/pallas_call | solution.py:406
  50.4 2.8 %shrink_outer.1 = (bf16[2,2,2,2,192,384]{5,4,3,2,1,0:T(8,128)(2,1)S(1)}, bf16[2,2,2,96,384]{4,3,2,1,0:T(8,128)(2,1)S(1)}, bf16[2,2,2,96,384]{4,3,2,1,0:T(8,128)(2,1)S(1)}) custom-call(s32[4]{0:T(128)S(1)} %pad_add_fusion.refs_0_.place_ref, bf16[256,1536]{1,0:T(8,128)(2,1)S(1)} %get-tuple-element.163.hidden_ref, ...), custom_call_target="tpu_custom_call" | custom-call | flops 2147483648 | bytes 10485760 | tf_op jit(solution)/shard_map/shrink_outer/pallas_call | solution.py:663
  55.3 7.1 %turn.1 = (bf16[256,3072]{1,0:T(8,128)(2,1)S(1)}, bf16[256,768]{1,0:T(8,128)(2,1)S(1)}, f32[256,768]{1,0:T(8,128)S(1)}, f32[1,4608]{1,0:T(1,128)S(1)}, bf16[128,...) custom-call(s32[4]{0:T(128)S(1)} %pad_add_fusion.refs_0_.place_ref, ...), custom_call_target="tpu_custom_call" | custom-call | flops 9663676416 | bytes 8388608 | tf_op jit(solution)/shard_map/turn/pallas_call | solution.py:558
  62.4 6.4 %collective-permute-done.26.refs_1_ = bf16[2,2,2,96,384]{4,3,2,1,0:T(8,128)(2,1)S(1)} collective-permute-done((bf16[2,2,2,96,384]{4,3,2,1,0:T(8,128)(2,1)S(1)}, bf16[2,2,2,96,384]{4,3,2,1,0:T(8,128)(2,1)S(1)}, u32[]{:S(2)}, u32[]{:S(2)}) %collective-permute-start.26) | collective-permute-done | bytes 589856 | tf_op jit(solution)/shard_map/ppermute | solution.py:787
  77.4 3.0 %expand_outer.1 = (bf16[2,2,2,2,48,1920]{5,4,3,2,1,0:T(8,128)(2,1)S(1)}, bf16[2,2,2,48,1024]{4,3,2,1,0:T(8,128)(2,1)S(1)}, bf16[2,2,2,48,896]{4,3,2,1,0:T(8,128)(2,1)S(1)}) custom-call(s32[4]{0:T(128)S(1)} %pad_add_fusion.refs_0_.place_ref, bf16[256,768]{1,0:T(8,128)(2,1)S(1)} %get-tuple-element.167.second_ref, ...), custom_call_target="tpu_custom_call" | custom-call | flops 2147483648 | bytes 10485760 | tf_op jit(solution)/shard_map/expand_outer/pallas_call | solution.py:663
  82.2 1.9 %collective-permute-done.32.refs_2_ = bf16[2,2,96,384]{3,2,1,0:T(8,128)(2,1)S(1)} collective-permute-done((bf16[2,2,96,384]{3,2,1,0:T(8,128)(2,1)S(1)}, bf16[2,2,96,384]{3,2,1,0:T(8,128)(2,1)S(1)}, u32[]{:S(2)}, u32[]{:S(2)}) %collective-permute-start.32) | collective-permute-done | bytes 294944 | tf_op jit(solution)/shard_map/ppermute | solution.py:787
  87.4 1.8 %collective-permute-start.38 = (bf16[64,768]{1,0:T(8,128)(2,1)S(1)}, bf16[64,768]{1,0:T(8,128)(2,1)S(1)}, u32[]{:S(2)}, u32[]{:S(2)}) collective-permute-start(bf16[64,768]{1,0:T(8,128)(2,1)S(1)} %get-tuple-element.210), channel_id=1, source_target_pairs={{0,8},{1,9},{2,10},{3,11},{4,12},{5,13},{6,14},{7,15},{8,0},{9,1},... | collective-permute-start | bytes 294920 | tf_op jit(solution)/shard_map/ppermute | solution.py:787
  90.0 11.7 %attention_backward.1 = (bf16[8,48,576]{2,1,0:T(8,128)(2,1)S(1)}, bf16[9,48,576]{2,1,0:T(8,128)(2,1)S(1)}, bf16[2,256,768]{2,1,0:T(8,128)(2,1)S(1)}, bf16[2,256,768]{2,1,0:T(8,128)(2,1)S(1)}) custom-call(s32[4]{0:T(128)S(1)} %pad_add_fusion.refs_0_.place_ref, bf16[1024,768]{1,0:T(8,128)(2,1)S(1)} %get-tuple-element.132.refs_1_, ...), custom_call_target="tpu_custom_call" | custom-call | flops 10737418240 | bytes 10485760 | tf_op jit(solution)/shard_map/attention_backward/pallas_call | solution.py:285
  103.1 1.8 %collective-permute-done.35.refs_1_ = bf16[2,2,2,48,1024]{4,3,2,1,0:T(8,128)(2,1)S(1)} collective-permute-done((bf16[2,2,2,48,1024]{4,3,2,1,0:T(8,128)(2,1)S(1)}, bf16[2,2,2,48,1024]{4,3,2,1,0:T(8,128)(2,1)S(1)}, u32[]{:S(2)}, u32[]{:S(2)}) %collective-permute-start.35) | collective-permute-done | bytes 786464 | tf_op jit(solution)/shard_map/ppermute | solution.py:787
  108.5 1.9 %collective-permute-start.45 = (bf16[192,384]{1,0:T(8,128)(2,1)S(1)}, bf16[192,384]{1,0:T(8,128)(2,1)S(1)}, u32[]{:S(2)}, u32[]{:S(2)}) collective-permute-start(bf16[192,384]{1,0:T(8,128)(2,1)S(1)} %plane_halves.5), channel_id=1, source_target_pairs={{0,8},{1,9},{2,10},{3,11},{4,12},{5,13},{6,14},{7,15},{8,0},{9,1},... | collective-permute-start | bytes 442376 | tf_op jit(solution)/shard_map/ppermute | solution.py:787
  110.4 10.5 %collective-permute-done.45.refs_4_ = bf16[192,384]{1,0:T(8,128)(2,1)S(1)} collective-permute-done((bf16[192,384]{1,0:T(8,128)(2,1)S(1)}, bf16[192,384]{1,0:T(8,128)(2,1)S(1)}, u32[]{:S(2)}, u32[]{:S(2)}) %collective-permute-start.45) | collective-permute-done | bytes 147488 | tf_op jit(solution)/shard_map/ppermute | solution.py:787
  121.0 2.1 %collective-permute-done.41.refs_1_ = bf16[9,48,576]{2,1,0:T(8,128)(2,1)S(1)} collective-permute-done((bf16[9,48,576]{2,1,0:T(8,128)(2,1)S(1)}, bf16[9,48,576]{2,1,0:T(8,128)(2,1)S(1)}, u32[]{:S(2)}, u32[]{:S(2)}) %collective-permute-start.41) | collective-permute-done | bytes 497696 | tf_op jit(solution)/shard_map/ppermute | solution.py:787
  123.1 2.2 %collective-permute-done.42.refs_8_ = bf16[256,768]{1,0:T(8,128)(2,1)S(1)} collective-permute-done((bf16[256,768]{1,0:T(8,128)(2,1)S(1)}, bf16[256,768]{1,0:T(8,128)(2,1)S(1)}, u32[]{:S(2)}, u32[]{:S(2)}) %collective-permute-start.42) | collective-permute-done | bytes 393248 | tf_op jit(solution)/shard_map/ppermute | solution.py:787
  125.3 2.0 %collective-permute-start.49 = (bf16[5,48,576]{2,1,0:T(8,128)(2,1)S(1)}, bf16[5,48,576]{2,1,0:T(8,128)(2,1)S(1)}, u32[]{:S(2)}, u32[]{:S(2)}) collective-permute-start(bf16[5,48,576]{2,1,0:T(8,128)(2,1)S(1)} %joined_halves.1.refs_3_), channel_id=1, source_target_pairs={{0,8},{1,9},{2,10},{3,11},{4,12},{5,13},{6,14},{7,15},{8,0},{9,1},... | collective-permute-start | bytes 829448 | tf_op jit(solution)/shard_map/ppermute | solution.py:787
  129.1 12.5 %collective-permute-done.49.refs_2_ = bf16[5,48,576]{2,1,0:T(8,128)(2,1)S(1)} collective-permute-done((bf16[5,48,576]{2,1,0:T(8,128)(2,1)S(1)}, bf16[5,48,576]{2,1,0:T(8,128)(2,1)S(1)}, u32[]{:S(2)}, u32[]{:S(2)}) %collective-permute-start.49) | collective-permute-done | bytes 276512 | tf_op jit(solution)/shard_map/ppermute | solution.py:787
  145.3 2.0 %collective-permute-start.46 = (bf16[64,768]{1,0:T(8,128)(2,1)S(1)}, bf16[64,768]{1,0:T(8,128)(2,1)S(1)}, u32[]{:S(2)}, u32[]{:S(2)}) collective-permute-start(bf16[64,768]{1,0:T(8,128)(2,1)S(1)} %get-tuple-element.228), channel_id=1, source_target_pairs={{0,4},{1,5},{2,6},{3,7},{4,0},{5,1},{6,2},{7,3},{8,12},{9,13},{10,... | collective-permute-start | bytes 294920 | tf_op jit(solution)/shard_map/ppermute | solution.py:787
  147.7 2.1 %collective-permute-start.48 = (bf16[64,768]{1,0:T(8,128)(2,1)S(1)}, bf16[64,768]{1,0:T(8,128)(2,1)S(1)}, u32[]{:S(2)}, u32[]{:S(2)}) collective-permute-start(bf16[64,768]{1,0:T(8,128)(2,1)S(1)} %get-tuple-element.230), channel_id=1, source_target_pairs={{0,12},{1,13},{2,14},{3,15},{4,8},{5,9},{6,10},{7,11},{8,4},{9,5},... | collective-permute-start | bytes 294920 | tf_op jit(solution)/shard_map/ppermute | solution.py:787
  151.5 8.2 %collective-permute-done.47.refs_2_ = bf16[64,768]{1,0:T(8,128)(2,1)S(1)} collective-permute-done((bf16[64,768]{1,0:T(8,128)(2,1)S(1)}, bf16[64,768]{1,0:T(8,128)(2,1)S(1)}, u32[]{:S(2)}, u32[]{:S(2)}) %collective-permute-start.47) | collective-permute-done | bytes 98336 | tf_op jit(solution)/shard_map/ppermute | solution.py:787
  (145 shorter events, 61.9 us)
Async XLA Ops:
  1.8 15.8 %collective-permute-start.1 = (bf16[64,768]{1,0:T(8,128)(2,1)S(1)}, bf16[64,768]{1,0:T(8,128)(2,1)S(1)}, u32[]{:S(2)}, u32[]{:S(2)}) collective-permute-start(bf16[64,768]{1,0:T(8,128)(2,1)S(1)} %get-tuple-element.255.refs_4_.refs_5_.refs_0_), channel_id=1, source_target_pairs={{0,1},{1,0},{2,3},{3,2},{4,5},{5,4},{6,7},{7,6},{8,9},{9,8},{10,11... | collective-permute-start | bytes 294920 | tf_op jit(solution)/shard_map/ppermute | solution.py:787
  2.3 11.6 %collective-permute-start.2 = (bf16[64,768]{1,0:T(8,128)(2,1)S(1)}, bf16[64,768]{1,0:T(8,128)(2,1)S(1)}, u32[]{:S(2)}, u32[]{:S(2)}) collective-permute-start(bf16[64,768]{1,0:T(8,128)(2,1)S(1)} %get-tuple-element.255.refs_4_.refs_5_.refs_0_), channel_id=1, source_target_pairs={{0,2},{1,3},{2,0},{3,1},{4,6},{5,7},{6,4},{7,5},{8,10},{9,11},{10,... | collective-permute-start | bytes 294920 | tf_op jit(solution)/shard_map/ppermute | solution.py:787
  35.2 12.0 %collective-permute-start.18 = (bf16[64,768]{1,0:T(8,128)(2,1)S(1)}, bf16[64,768]{1,0:T(8,128)(2,1)S(1)}, u32[]{:S(2)}, u32[]{:S(2)}) collective-permute-start(bf16[64,768]{1,0:T(8,128)(2,1)S(1)} %get-tuple-element.252), channel_id=1, source_target_pairs={{0,4},{1,5},{2,6},{3,7},{4,0},{5,1},{6,2},{7,3},{8,12},{9,13},{10,... | collective-permute-start | bytes 294920 | tf_op jit(solution)/shard_map/ppermute | solution.py:787
  48.7 13.6 %collective-permute-start.28 = (bf16[256,768]{1,0:T(8,128)(2,1)S(1)}, bf16[256,768]{1,0:T(8,128)(2,1)S(1)}, u32[]{:S(2)}, u32[]{:S(2)}) collective-permute-start(bf16[256,768]{1,0:T(8,128)(2,1)S(1)} %get-tuple-element.167.second_ref), channel_id=1, source_target_pairs={{0,1},{1,0},{2,3},{3,2},{4,5},{5,4},{6,7},{7,6},{8,9},{9,8},{10,11... | collective-permute-start | bytes 1179656 | tf_op jit(solution)/shard_map/ppermute | solution.py:787
  49.0 13.4 %collective-permute-start.29 = (bf16[256,768]{1,0:T(8,128)(2,1)S(1)}, bf16[256,768]{1,0:T(8,128)(2,1)S(1)}, u32[]{:S(2)}, u32[]{:S(2)}) collective-permute-start(bf16[256,768]{1,0:T(8,128)(2,1)S(1)} %get-tuple-element.168.mixed_ref), channel_id=1, source_target_pairs={{0,1},{1,0},{2,3},{3,2},{4,5},{5,4},{6,7},{7,6},{8,9},{9,8},{10,11... | collective-permute-start | bytes 1179656 | tf_op jit(solution)/shard_map/ppermute | solution.py:787
  53.2 15.5 %collective-permute-start.26 = (bf16[2,2,2,96,384]{4,3,2,1,0:T(8,128)(2,1)S(1)}, bf16[2,2,2,96,384]{4,3,2,1,0:T(8,128)(2,1)S(1)}, u32[]{:S(2)}, u32[]{:S(2)}) collective-permute-start(bf16[2,2,2,96,384]{4,3,2,1,0:T(8,128)(2,1)S(1)} %get-tuple-element.165), channel_id=1, source_target_pairs={{0,16},{16,0},{1,17},{17,1},{2,18},{18,2},{3,19},{19,3},{4,20},{20... | collective-permute-start | bytes 1769480 | tf_op jit(solution)/shard_map/ppermute | solution.py:787
  54.8 15.2 %collective-permute-start.27 = (bf16[2,2,2,96,384]{4,3,2,1,0:T(8,128)(2,1)S(1)}, bf16[2,2,2,96,384]{4,3,2,1,0:T(8,128)(2,1)S(1)}, u32[]{:S(2)}, u32[]{:S(2)}) collective-permute-start(bf16[2,2,2,96,384]{4,3,2,1,0:T(8,128)(2,1)S(1)} %get-tuple-element.166), channel_id=1, source_target_pairs={{0,2},{1,3},{2,0},{3,1},{4,6},{5,7},{6,4},{7,5},{8,10},{9,11},{10,... | collective-permute-start | bytes 1769480 | tf_op jit(solution)/shard_map/ppermute | solution.py:787
  84.5 17.3 %collective-permute-start.34 = (bf16[2,192,384]{2,1,0:T(8,128)(2,1)S(1)}, bf16[2,192,384]{2,1,0:T(8,128)(2,1)S(1)}, u32[]{:S(2)}, u32[]{:S(2)}) collective-permute-start(bf16[2,192,384]{2,1,0:T(8,128)(2,1)S(1)} %plane_halves.4), channel_id=1, source_target_pairs={{0,4},{1,5},{2,6},{3,7},{4,0},{5,1},{6,2},{7,3},{8,12},{9,13},{10,... | collective-permute-start | bytes 884744 | tf_op jit(solution)/shard_map/ppermute | solution.py:787
  86.3 18.7 %collective-permute-start.35 = (bf16[2,2,2,48,1024]{4,3,2,1,0:T(8,128)(2,1)S(1)}, bf16[2,2,2,48,1024]{4,3,2,1,0:T(8,128)(2,1)S(1)}, u32[]{:S(2)}, u32[]{:S(2)}) collective-permute-start(bf16[2,2,2,48,1024]{4,3,2,1,0:T(8,128)(2,1)S(1)} %get-tuple-element.206), channel_id=1, source_target_pairs={{0,16},{16,0},{1,17},{17,1},{2,18},{18,2},{3,19},{19,3},{4,20},{20... | collective-permute-start | bytes 2359304 | tf_op jit(solution)/shard_map/ppermute | solution.py:787
  86.8 16.3 %collective-permute-start.36 = (bf16[2,2,2,48,896]{4,3,2,1,0:T(8,128)(2,1)S(1)}, bf16[2,2,2,48,896]{4,3,2,1,0:T(8,128)(2,1)S(1)}, u32[]{:S(2)}, u32[]{:S(2)}) collective-permute-start(bf16[2,2,2,48,896]{4,3,2,1,0:T(8,128)(2,1)S(1)} %get-tuple-element.207), channel_id=1, source_target_pairs={{0,2},{1,3},{2,0},{3,1},{4,6},{5,7},{6,4},{7,5},{8,10},{9,11},{10,... | collective-permute-start | bytes 2064392 | tf_op jit(solution)/shard_map/ppermute | solution.py:787
  87.4 14.4 %collective-permute-start.38 = (bf16[64,768]{1,0:T(8,128)(2,1)S(1)}, bf16[64,768]{1,0:T(8,128)(2,1)S(1)}, u32[]{:S(2)}, u32[]{:S(2)}) collective-permute-start(bf16[64,768]{1,0:T(8,128)(2,1)S(1)} %get-tuple-element.210), channel_id=1, source_target_pairs={{0,8},{1,9},{2,10},{3,11},{4,12},{5,13},{6,14},{7,15},{8,0},{9,1},... | collective-permute-start | bytes 294920 | tf_op jit(solution)/shard_map/ppermute | solution.py:787
  89.2 12.5 %collective-permute-start.39 = (bf16[64,768]{1,0:T(8,128)(2,1)S(1)}, bf16[64,768]{1,0:T(8,128)(2,1)S(1)}, u32[]{:S(2)}, u32[]{:S(2)}) collective-permute-start(bf16[64,768]{1,0:T(8,128)(2,1)S(1)} %get-tuple-element.211), channel_id=1, source_target_pairs={{0,12},{1,13},{2,14},{3,15},{4,8},{5,9},{6,10},{7,11},{8,4},{9,5},... | collective-permute-start | bytes 294920 | tf_op jit(solution)/shard_map/ppermute | solution.py:787
  105.0 18.1 %collective-permute-start.41 = (bf16[9,48,576]{2,1,0:T(8,128)(2,1)S(1)}, bf16[9,48,576]{2,1,0:T(8,128)(2,1)S(1)}, u32[]{:S(2)}, u32[]{:S(2)}) collective-permute-start(bf16[9,48,576]{2,1,0:T(8,128)(2,1)S(1)} %get-tuple-element.219.refs_2_), channel_id=1, source_target_pairs={{0,4},{1,5},{2,6},{3,7},{4,0},{5,1},{6,2},{7,3},{8,12},{9,13},{10,... | collective-permute-start | bytes 1493000 | tf_op jit(solution)/shard_map/ppermute | solution.py:787
  105.5 15.5 %collective-permute-start.43 = (bf16[2,2,48,1024]{3,2,1,0:T(8,128)(2,1)S(1)}, bf16[2,2,48,1024]{3,2,1,0:T(8,128)(2,1)S(1)}, u32[]{:S(2)}, u32[]{:S(2)}) collective-permute-start(bf16[2,2,48,1024]{3,2,1,0:T(8,128)(2,1)S(1)} %get-tuple-element.223), channel_id=1, source_target_pairs={{0,2},{1,3},{2,0},{3,1},{4,6},{5,7},{6,4},{7,5},{8,10},{9,11},{10,... | collective-permute-start | bytes 1179656 | tf_op jit(solution)/shard_map/ppermute | solution.py:787
  107.4 17.9 %collective-permute-start.42 = (bf16[256,768]{1,0:T(8,128)(2,1)S(1)}, bf16[256,768]{1,0:T(8,128)(2,1)S(1)}, u32[]{:S(2)}, u32[]{:S(2)}) collective-permute-start(bf16[256,768]{1,0:T(8,128)(2,1)S(1)} %branch_halves.1), channel_id=1, source_target_pairs={{0,2},{1,3},{2,0},{3,1},{4,6},{5,7},{6,4},{7,5},{8,10},{9,11},{10,... | collective-permute-start | bytes 1179656 | tf_op jit(solution)/shard_map/ppermute | solution.py:787
  107.9 13.0 %collective-permute-start.44 = (bf16[2,2,48,896]{3,2,1,0:T(8,128)(2,1)S(1)}, bf16[2,2,48,896]{3,2,1,0:T(8,128)(2,1)S(1)}, u32[]{:S(2)}, u32[]{:S(2)}) collective-permute-start(bf16[2,2,48,896]{3,2,1,0:T(8,128)(2,1)S(1)} %get-tuple-element.224), channel_id=1, source_target_pairs={{0,16},{16,0},{1,17},{17,1},{2,18},{18,2},{3,19},{19,3},{4,20},{20... | collective-permute-start | bytes 1032200 | tf_op jit(solution)/shard_map/ppermute | solution.py:787
  108.5 12.4 %collective-permute-start.45 = (bf16[192,384]{1,0:T(8,128)(2,1)S(1)}, bf16[192,384]{1,0:T(8,128)(2,1)S(1)}, u32[]{:S(2)}, u32[]{:S(2)}) collective-permute-start(bf16[192,384]{1,0:T(8,128)(2,1)S(1)} %plane_halves.5), channel_id=1, source_target_pairs={{0,8},{1,9},{2,10},{3,11},{4,12},{5,13},{6,14},{7,15},{8,0},{9,1},... | collective-permute-start | bytes 442376 | tf_op jit(solution)/shard_map/ppermute | solution.py:787
  125.3 16.2 %collective-permute-start.49 = (bf16[5,48,576]{2,1,0:T(8,128)(2,1)S(1)}, bf16[5,48,576]{2,1,0:T(8,128)(2,1)S(1)}, u32[]{:S(2)}, u32[]{:S(2)}) collective-permute-start(bf16[5,48,576]{2,1,0:T(8,128)(2,1)S(1)} %joined_halves.1.refs_3_), channel_id=1, source_target_pairs={{0,8},{1,9},{2,10},{3,11},{4,12},{5,13},{6,14},{7,15},{8,0},{9,1},... | collective-permute-start | bytes 829448 | tf_op jit(solution)/shard_map/ppermute | solution.py:787
  127.5 15.3 %collective-permute-start.54 = (bf16[2,48,1920]{2,1,0:T(8,128)(2,1)S(1)}, bf16[2,48,1920]{2,1,0:T(8,128)(2,1)S(1)}, u32[]{:S(2)}, u32[]{:S(2)}) collective-permute-start(bf16[2,48,1920]{2,1,0:T(8,128)(2,1)S(1)} %plane_halves.6), channel_id=1, source_target_pairs={{0,4},{1,5},{2,6},{3,7},{4,0},{5,1},{6,2},{7,3},{8,12},{9,13},{10,... | collective-permute-start | bytes 1105928 | tf_op jit(solution)/shard_map/ppermute | solution.py:787
  142.9 17.3 %collective-permute-start.55 = (bf16[48,1920]{1,0:T(8,128)(2,1)S(1)}, bf16[48,1920]{1,0:T(8,128)(2,1)S(1)}, u32[]{:S(2)}, u32[]{:S(2)}) collective-permute-start(bf16[48,1920]{1,0:T(8,128)(2,1)S(1)} %plane_halves.7), channel_id=1, source_target_pairs={{0,8},{1,9},{2,10},{3,11},{4,12},{5,13},{6,14},{7,15},{8,0},{9,1},... | collective-permute-start | bytes 552968 | tf_op jit(solution)/shard_map/ppermute | solution.py:787
  147.3 12.4 %collective-permute-start.47 = (bf16[64,768]{1,0:T(8,128)(2,1)S(1)}, bf16[64,768]{1,0:T(8,128)(2,1)S(1)}, u32[]{:S(2)}, u32[]{:S(2)}) collective-permute-start(bf16[64,768]{1,0:T(8,128)(2,1)S(1)} %get-tuple-element.229), channel_id=1, source_target_pairs={{0,8},{1,9},{2,10},{3,11},{4,12},{5,13},{6,14},{7,15},{8,0},{9,1},... | collective-permute-start | bytes 294920 | tf_op jit(solution)/shard_map/ppermute | solution.py:787
  147.7 12.6 %collective-permute-start.48 = (bf16[64,768]{1,0:T(8,128)(2,1)S(1)}, bf16[64,768]{1,0:T(8,128)(2,1)S(1)}, u32[]{:S(2)}, u32[]{:S(2)}) collective-permute-start(bf16[64,768]{1,0:T(8,128)(2,1)S(1)} %get-tuple-element.230), channel_id=1, source_target_pairs={{0,12},{1,13},{2,14},{3,15},{4,8},{5,9},{6,10},{7,11},{8,4},{9,5},... | collective-permute-start | bytes 294920 | tf_op jit(solution)/shard_map/ppermute | solution.py:787
  149.9 14.7 %collective-permute-start.57 = (bf16[192,384]{1,0:T(8,128)(2,1)S(1)}, bf16[192,384]{1,0:T(8,128)(2,1)S(1)}, u32[]{:S(2)}, u32[]{:S(2)}) collective-permute-start(bf16[192,384]{1,0:T(8,128)(2,1)S(1)} %last_halves.3.own_ref), channel_id=1, source_target_pairs={{0,16},{16,0},{1,17},{17,1},{2,18},{18,2},{3,19},{19,3},{4,20},{20... | collective-permute-start | bytes 442376 | tf_op jit(solution)/shard_map/ppermute | solution.py:787
  151.5 14.5 %collective-permute-start.51 = (bf16[2,48,576]{2,1,0:T(8,128)(2,1)S(1)}, bf16[2,48,576]{2,1,0:T(8,128)(2,1)S(1)}, u32[]{:S(2)}, u32[]{:S(2)}) collective-permute-start(bf16[2,48,576]{2,1,0:T(8,128)(2,1)S(1)} %get-tuple-element.234), channel_id=1, source_target_pairs={{0,1},{1,0},{2,3},{3,2},{4,5},{5,4},{6,7},{7,6},{8,9},{9,8},{10,11... | collective-permute-start | bytes 331784 | tf_op jit(solution)/shard_map/ppermute | solution.py:787
  (42 other events, 358.0 us)
where the time goes:
time: 171 us; the launch traced here: 170 us
  waiting for transfers between devices  65.1 us (38%)
  Pallas kernels  49 us (29%)
  starting transfers between devices  48.2 us (28%)
  local copies, waits for them, and re-layouts  6.48 us (4%)
    ppermute x58, waiting for transfers between devices, swap(): return lax.ppermute(value, axis, [(i, i ^ bits) for i in range(size)])  65.1 us
    ppermute x58, starting transfers between devices, swap(): return lax.ppermute(value, axis, [(i, i ^ bits) for i in range(size)])  48.2 us
    pallas_call x1, Pallas kernels, backward_call(): pl.pallas_call(kernel, out_shape=(jax.ShapeDtypeStruct((planes * slots //...  11.7 us
    pallas_call x1, Pallas kernels, forward_call(): pl.pallas_call(kernel, out_shape=(pltpu.VMEM((length, width), bf16), pltp...  7.76 us
    pallas_call x1, Pallas kernels, turn_call(): pl.pallas_call(functools.partial(turn_kernel, slots=slots, planes=planes,...  7.09 us
    pallas_call x1, Pallas kernels, widen_call(): pl.pallas_call(functools.partial(widen_kernel, slots=slots, planes=len(in...  7.07 us
    pallas_call x2, Pallas kernels, outer_call(): pl.pallas_call(functools.partial(kernel, cutting=dict(bands=bands, steps=...  5.76 us
  transfers between devices with their start and end apart: 58, of which 26 were waited for; matrix products, arithmetic and copies ran while one was open for 3% of the time, Pallas kernels for 23%

commit v1 on v0

--- a/solution.py
+++ b/solution.py
@@ -261,10 +261,11 @@
                 pl.ds(pl.multiple_of(offset, rows_each), rows_each), :
             ].astype(bf16)
             at += 1
-    joined_give[half] = jnp.zeros((rows_each, wide), bf16)
+    outer_ref[:rows_each, :] = jnp.zeros((rows_each, wide), f32)
     for r in range(-(-gains // wide)):
         end = min((r + 1) * wide, gains)
-        joined_give[half, r : r + 1, : end - r * wide] = row_ref[:, r * wide : end].astype(bf16)
+        outer_ref[r : r + 1, : end - r * wide] = row_ref[:, r * wide : end]
+    joined_give[half] = outer_ref[:rows_each, :].astype(bf16)
 
 
 def backward_call(

time: 171 us -> 171 us (level)
  no operation moved by 1% of the time
where the time goes in v1:
time: 171 us; the launch traced here: 170 us
  waiting for transfers between devices  65.1 us (38%)
  Pallas kernels  49 us (29%)
  starting transfers between devices  48.2 us (28%)
  local copies, waits for them, and re-layouts  6.48 us (4%)
    ppermute x58, waiting for transfers between devices, swap(): return lax.ppermute(value, axis, [(i, i ^ bits) for i in range(size)])  65.1 us
    ppermute x58, starting transfers between devices, swap(): return lax.ppermute(value, axis, [(i, i ^ bits) for i in range(size)])  48.2 us
    pallas_call x1, Pallas kernels, backward_call(): pl.pallas_call(kernel, out_shape=(jax.ShapeDtypeStruct((planes * slots //...  11.7 us
    pallas_call x1, Pallas kernels, forward_call(): pl.pallas_call(kernel, out_shape=(pltpu.VMEM((length, width), bf16), pltp...  7.76 us
    pallas_call x1, Pallas kernels, turn_call(): pl.pallas_call(functools.partial(turn_kernel, slots=slots, planes=planes,...  7.09 us
    pallas_call x1, Pallas kernels, widen_call(): pl.pallas_call(functools.partial(widen_kernel, slots=slots, planes=len(in...  7.07 us
    pallas_call x2, Pallas kernels, outer_call(): pl.pallas_call(functools.partial(kernel, cutting=dict(bands=bands, steps=...  5.76 us
  transfers between devices with their start and end apart: 58, of which 26 were waited for; matrix products, arithmetic and copies ran while one was open for 3% of the time, Pallas kernels for 23%

profile of v1, /device:TPU:0, one launch (start us, length us, event | category | flops | bytes accessed | tf_op | source)
XLA Modules:
  0.0 170.2 jit_solution(12017958950058680343)
XLA Ops:
  2.3 2.6 %collective-permute-start.2 = (bf16[64,768]{1,0:T(8,128)(2,1)S(1)}, bf16[64,768]{1,0:T(8,128)(2,1)S(1)}, u32[]{:S(2)}, u32[]{:S(2)}) collective-permute-start(bf16[64,768]{1,0:T(8,128)(2,1)S(1)} %get-tuple-element.255.refs_4_.refs_5_.refs_0_), channel_id=1, source_target_pairs={{0,2},{1,3},{2,0},{3,1},{4,6},{5,7},{6,4},{7,5},{8,10},{9,11},{10,... | collective-permute-start | bytes 294920 | tf_op jit(solution)/shard_map/ppermute | solution.py:788
  4.9 3.6 %collective-permute-start = (bf16[64,768]{1,0:T(8,128)(2,1)S(1)}, bf16[64,768]{1,0:T(8,128)(2,1)S(1)}, u32[]{:S(2)}, u32[]{:S(2)}) collective-permute-start(bf16[64,768]{1,0:T(8,128)(2,1)S(1)} %get-tuple-element.256), channel_id=1, source_target_pairs={{0,12},{1,13},{2,14},{3,15},{4,8},{5,9},{6,10},{7,11},{8,4},{9,5},... | collective-permute-start | bytes 294920 | tf_op jit(solution)/shard_map/ppermute | solution.py:788
  11.4 2.0 %constant_dynamic-slice_fusion.2 = (bf16[768,192]{1,0:T(8,128)(2,1)S(1)}, bf16[768,192]{1,0:T(8,128)(2,1)S(1)}, bf16[768,192]{1,0:T(8,128)(2,1)S(1)}) fusion(bf16[768,2304]{1,0:T(8,128)(2,1)} %param.14, s32[]{:T(128)S(6)} %select_n.45, s32[]{:T(128)S(6)} %select_n.47, s32[]{:T(128)S(6)} %select_n.46), kind=kLoop, calls=%fused_computation.14 | loop fusion | bytes 1769484 | tf_op jit(solution)/shard_map/dynamic_slice | solution.py:932
  20.4 2.4 %collective-permute-done.10.refs_14_ = bf16[64,768]{1,0:T(8,128)(2,1)S(1)} collective-permute-done((bf16[64,768]{1,0:T(8,128)(2,1)S(1)}, bf16[64,768]{1,0:T(8,128)(2,1)S(1)}, u32[]{:S(2)}, u32[]{:S(2)}) %collective-permute-start.10) | collective-permute-done | bytes 98336 | tf_op jit(solution)/shard_map/ppermute | solution.py:788
  25.5 7.8 %attention_forward.1 = (bf16[1024,768]{1,0:T(8,128)(2,1)S(1)}, bf16[9,1024,64]{2,1,0:T(8,128)(2,1)S(1)}, f32[1024,3]{1,0:T(8,128)S(1)}, bf16[128,384]{1,0:T(8,12...) custom-call(s32[4]{0:T(128)S(1)} %pad_add_fusion.refs_0_.place_ref, ...), custom_call_target="tpu_custom_call" | custom-call | flops 8589934592 | bytes 8388608 | tf_op jit(solution)/shard_map/attention_forward/pallas_call | solution.py:163
  36.8 1.9 %collective-permute-start.19 = (bf16[64,768]{1,0:T(8,128)(2,1)S(1)}, bf16[64,768]{1,0:T(8,128)(2,1)S(1)}, u32[]{:S(2)}, u32[]{:S(2)}) collective-permute-start(bf16[64,768]{1,0:T(8,128)(2,1)S(1)} %get-tuple-element.251), channel_id=1, source_target_pairs={{0,8},{1,9},{2,10},{3,11},{4,12},{5,13},{6,14},{7,15},{8,0},{9,1},... | collective-permute-start | bytes 294920 | tf_op jit(solution)/shard_map/ppermute | solution.py:788
  40.1 7.1 %widen.1 = (bf16[256,768]{1,0:T(8,128)(2,1)S(1)}, f32[256,768]{1,0:T(8,128)S(1)}, bf16[256,768]{1,0:T(8,128)(2,1)S(1)}, bf16[256,1536]{1,0:T(8,128)(2,1)S(1)}, b...) custom-call(s32[4]{0:T(128)S(1)} %pad_add_fusion.refs_0_.place_ref, ...), custom_call_target="tpu_custom_call" | custom-call | flops 6442450944 | bytes 6291456 | tf_op jit(solution)/shard_map/widen/pallas_call | solution.py:407
  50.4 2.8 %shrink_outer.1 = (bf16[2,2,2,2,192,384]{5,4,3,2,1,0:T(8,128)(2,1)S(1)}, bf16[2,2,2,96,384]{4,3,2,1,0:T(8,128)(2,1)S(1)}, bf16[2,2,2,96,384]{4,3,2,1,0:T(8,128)(2,1)S(1)}) custom-call(s32[4]{0:T(128)S(1)} %pad_add_fusion.refs_0_.place_ref, bf16[256,1536]{1,0:T(8,128)(2,1)S(1)} %get-tuple-element.163.hidden_ref, ...), custom_call_target="tpu_custom_call" | custom-call | flops 2147483648 | bytes 10485760 | tf_op jit(solution)/shard_map/shrink_outer/pallas_call | solution.py:664
  55.3 7.1 %turn.1 = (bf16[256,3072]{1,0:T(8,128)(2,1)S(1)}, bf16[256,768]{1,0:T(8,128)(2,1)S(1)}, f32[256,768]{1,0:T(8,128)S(1)}, f32[1,4608]{1,0:T(1,128)S(1)}, bf16[128,...) custom-call(s32[4]{0:T(128)S(1)} %pad_add_fusion.refs_0_.place_ref, ...), custom_call_target="tpu_custom_call" | custom-call | flops 9663676416 | bytes 8388608 | tf_op jit(solution)/shard_map/turn/pallas_call | solution.py:559
  62.4 6.4 %collective-permute-done.26.refs_1_ = bf16[2,2,2,96,384]{4,3,2,1,0:T(8,128)(2,1)S(1)} collective-permute-done((bf16[2,2,2,96,384]{4,3,2,1,0:T(8,128)(2,1)S(1)}, bf16[2,2,2,96,384]{4,3,2,1,0:T(8,128)(2,1)S(1)}, u32[]{:S(2)}, u32[]{:S(2)}) %collective-permute-start.26) | collective-permute-done | bytes 589856 | tf_op jit(solution)/shard_map/ppermute | solution.py:788
  77.4 3.0 %expand_outer.1 = (bf16[2,2,2,2,48,1920]{5,4,3,2,1,0:T(8,128)(2,1)S(1)}, bf16[2,2,2,48,1024]{4,3,2,1,0:T(8,128)(2,1)S(1)}, bf16[2,2,2,48,896]{4,3,2,1,0:T(8,128)(2,1)S(1)}) custom-call(s32[4]{0:T(128)S(1)} %pad_add_fusion.refs_0_.place_ref, bf16[256,768]{1,0:T(8,128)(2,1)S(1)} %get-tuple-element.167.second_ref, ...), custom_call_target="tpu_custom_call" | custom-call | flops 2147483648 | bytes 10485760 | tf_op jit(solution)/shard_map/expand_outer/pallas_call | solution.py:664
  82.2 1.9 %collective-permute-done.32.refs_2_ = bf16[2,2,96,384]{3,2,1,0:T(8,128)(2,1)S(1)} collective-permute-done((bf16[2,2,96,384]{3,2,1,0:T(8,128)(2,1)S(1)}, bf16[2,2,96,384]{3,2,1,0:T(8,128)(2,1)S(1)}, u32[]{:S(2)}, u32[]{:S(2)}) %collective-permute-start.32) | collective-permute-done | bytes 294944 | tf_op jit(solution)/shard_map/ppermute | solution.py:788
  87.4 1.8 %collective-permute-start.38 = (bf16[64,768]{1,0:T(8,128)(2,1)S(1)}, bf16[64,768]{1,0:T(8,128)(2,1)S(1)}, u32[]{:S(2)}, u32[]{:S(2)}) collective-permute-start(bf16[64,768]{1,0:T(8,128)(2,1)S(1)} %get-tuple-element.210), channel_id=1, source_target_pairs={{0,8},{1,9},{2,10},{3,11},{4,12},{5,13},{6,14},{7,15},{8,0},{9,1},... | collective-permute-start | bytes 294920 | tf_op jit(solution)/shard_map/ppermute | solution.py:788
  90.0 11.7 %attention_backward.1 = (bf16[8,48,576]{2,1,0:T(8,128)(2,1)S(1)}, bf16[9,48,576]{2,1,0:T(8,128)(2,1)S(1)}, bf16[2,256,768]{2,1,0:T(8,128)(2,1)S(1)}, bf16[2,256,768]{2,1,0:T(8,128)(2,1)S(1)}) custom-call(s32[4]{0:T(128)S(1)} %pad_add_fusion.refs_0_.place_ref, bf16[1024,768]{1,0:T(8,128)(2,1)S(1)} %get-tuple-element.132.refs_1_, ...), custom_call_target="tpu_custom_call" | custom-call | flops 10737418240 | bytes 10485760 | tf_op jit(solution)/shard_map/attention_backward/pallas_call | solution.py:286
  103.1 1.8 %collective-permute-done.35.refs_1_ = bf16[2,2,2,48,1024]{4,3,2,1,0:T(8,128)(2,1)S(1)} collective-permute-done((bf16[2,2,2,48,1024]{4,3,2,1,0:T(8,128)(2,1)S(1)}, bf16[2,2,2,48,1024]{4,3,2,1,0:T(8,128)(2,1)S(1)}, u32[]{:S(2)}, u32[]{:S(2)}) %collective-permute-start.35) | collective-permute-done | bytes 786464 | tf_op jit(solution)/shard_map/ppermute | solution.py:788
  108.5 1.9 %collective-permute-start.45 = (bf16[192,384]{1,0:T(8,128)(2,1)S(1)}, bf16[192,384]{1,0:T(8,128)(2,1)S(1)}, u32[]{:S(2)}, u32[]{:S(2)}) collective-permute-start(bf16[192,384]{1,0:T(8,128)(2,1)S(1)} %plane_halves.5), channel_id=1, source_target_pairs={{0,8},{1,9},{2,10},{3,11},{4,12},{5,13},{6,14},{7,15},{8,0},{9,1},... | collective-permute-start | bytes 442376 | tf_op jit(solution)/shard_map/ppermute | solution.py:788
  110.4 10.5 %collective-permute-done.45.refs_4_ = bf16[192,384]{1,0:T(8,128)(2,1)S(1)} collective-permute-done((bf16[192,384]{1,0:T(8,128)(2,1)S(1)}, bf16[192,384]{1,0:T(8,128)(2,1)S(1)}, u32[]{:S(2)}, u32[]{:S(2)}) %collective-permute-start.45) | collective-permute-done | bytes 147488 | tf_op jit(solution)/shard_map/ppermute | solution.py:788
  121.0 2.1 %collective-permute-done.41.refs_1_ = bf16[9,48,576]{2,1,0:T(8,128)(2,1)S(1)} collective-permute-done((bf16[9,48,576]{2,1,0:T(8,128)(2,1)S(1)}, bf16[9,48,576]{2,1,0:T(8,128)(2,1)S(1)}, u32[]{:S(2)}, u32[]{:S(2)}) %collective-permute-start.41) | collective-permute-done | bytes 497696 | tf_op jit(solution)/shard_map/ppermute | solution.py:788
  123.1 2.2 %collective-permute-done.42.refs_8_ = bf16[256,768]{1,0:T(8,128)(2,1)S(1)} collective-permute-done((bf16[256,768]{1,0:T(8,128)(2,1)S(1)}, bf16[256,768]{1,0:T(8,128)(2,1)S(1)}, u32[]{:S(2)}, u32[]{:S(2)}) %collective-permute-start.42) | collective-permute-done | bytes 393248 | tf_op jit(solution)/shard_map/ppermute | solution.py:788
  125.3 2.0 %collective-permute-start.49 = (bf16[5,48,576]{2,1,0:T(8,128)(2,1)S(1)}, bf16[5,48,576]{2,1,0:T(8,128)(2,1)S(1)}, u32[]{:S(2)}, u32[]{:S(2)}) collective-permute-start(bf16[5,48,576]{2,1,0:T(8,128)(2,1)S(1)} %joined_halves.1.refs_3_), channel_id=1, source_target_pairs={{0,8},{1,9},{2,10},{3,11},{4,12},{5,13},{6,14},{7,15},{8,0},{9,1},... | collective-permute-start | bytes 829448 | tf_op jit(solution)/shard_map/ppermute | solution.py:788
  129.1 12.5 %collective-permute-done.49.refs_2_ = bf16[5,48,576]{2,1,0:T(8,128)(2,1)S(1)} collective-permute-done((bf16[5,48,576]{2,1,0:T(8,128)(2,1)S(1)}, bf16[5,48,576]{2,1,0:T(8,128)(2,1)S(1)}, u32[]{:S(2)}, u32[]{:S(2)}) %collective-permute-start.49) | collective-permute-done | bytes 276512 | tf_op jit(solution)/shard_map/ppermute | solution.py:788
  145.3 2.0 %collective-permute-start.46 = (bf16[64,768]{1,0:T(8,128)(2,1)S(1)}, bf16[64,768]{1,0:T(8,128)(2,1)S(1)}, u32[]{:S(2)}, u32[]{:S(2)}) collective-permute-start(bf16[64,768]{1,0:T(8,128)(2,1)S(1)} %get-tuple-element.228), channel_id=1, source_target_pairs={{0,4},{1,5},{2,6},{3,7},{4,0},{5,1},{6,2},{7,3},{8,12},{9,13},{10,... | collective-permute-start | bytes 294920 | tf_op jit(solution)/shard_map/ppermute | solution.py:788
  147.7 2.1 %collective-permute-start.48 = (bf16[64,768]{1,0:T(8,128)(2,1)S(1)}, bf16[64,768]{1,0:T(8,128)(2,1)S(1)}, u32[]{:S(2)}, u32[]{:S(2)}) collective-permute-start(bf16[64,768]{1,0:T(8,128)(2,1)S(1)} %get-tuple-element.230), channel_id=1, source_target_pairs={{0,12},{1,13},{2,14},{3,15},{4,8},{5,9},{6,10},{7,11},{8,4},{9,5},... | collective-permute-start | bytes 294920 | tf_op jit(solution)/shard_map/ppermute | solution.py:788
  151.5 8.2 %collective-permute-done.47.refs_2_ = bf16[64,768]{1,0:T(8,128)(2,1)S(1)} collective-permute-done((bf16[64,768]{1,0:T(8,128)(2,1)S(1)}, bf16[64,768]{1,0:T(8,128)(2,1)S(1)}, u32[]{:S(2)}, u32[]{:S(2)}) %collective-permute-start.47) | collective-permute-done | bytes 98336 | tf_op jit(solution)/shard_map/ppermute | solution.py:788
  (145 shorter events, 61.9 us)
Async XLA Ops:
  1.8 15.8 %collective-permute-start.1 = (bf16[64,768]{1,0:T(8,128)(2,1)S(1)}, bf16[64,768]{1,0:T(8,128)(2,1)S(1)}, u32[]{:S(2)}, u32[]{:S(2)}) collective-permute-start(bf16[64,768]{1,0:T(8,128)(2,1)S(1)} %get-tuple-element.255.refs_4_.refs_5_.refs_0_), channel_id=1, source_target_pairs={{0,1},{1,0},{2,3},{3,2},{4,5},{5,4},{6,7},{7,6},{8,9},{9,8},{10,11... | collective-permute-start | bytes 294920 | tf_op jit(solution)/shard_map/ppermute | solution.py:788
  2.3 11.6 %collective-permute-start.2 = (bf16[64,768]{1,0:T(8,128)(2,1)S(1)}, bf16[64,768]{1,0:T(8,128)(2,1)S(1)}, u32[]{:S(2)}, u32[]{:S(2)}) collective-permute-start(bf16[64,768]{1,0:T(8,128)(2,1)S(1)} %get-tuple-element.255.refs_4_.refs_5_.refs_0_), channel_id=1, source_target_pairs={{0,2},{1,3},{2,0},{3,1},{4,6},{5,7},{6,4},{7,5},{8,10},{9,11},{10,... | collective-permute-start | bytes 294920 | tf_op jit(solution)/shard_map/ppermute | solution.py:788
  35.2 12.0 %collective-permute-start.18 = (bf16[64,768]{1,0:T(8,128)(2,1)S(1)}, bf16[64,768]{1,0:T(8,128)(2,1)S(1)}, u32[]{:S(2)}, u32[]{:S(2)}) collective-permute-start(bf16[64,768]{1,0:T(8,128)(2,1)S(1)} %get-tuple-element.252), channel_id=1, source_target_pairs={{0,4},{1,5},{2,6},{3,7},{4,0},{5,1},{6,2},{7,3},{8,12},{9,13},{10,... | collective-permute-start | bytes 294920 | tf_op jit(solution)/shard_map/ppermute | solution.py:788
  48.7 13.6 %collective-permute-start.28 = (bf16[256,768]{1,0:T(8,128)(2,1)S(1)}, bf16[256,768]{1,0:T(8,128)(2,1)S(1)}, u32[]{:S(2)}, u32[]{:S(2)}) collective-permute-start(bf16[256,768]{1,0:T(8,128)(2,1)S(1)} %get-tuple-element.167.second_ref), channel_id=1, source_target_pairs={{0,1},{1,0},{2,3},{3,2},{4,5},{5,4},{6,7},{7,6},{8,9},{9,8},{10,11... | collective-permute-start | bytes 1179656 | tf_op jit(solution)/shard_map/ppermute | solution.py:788
  49.0 13.4 %collective-permute-start.29 = (bf16[256,768]{1,0:T(8,128)(2,1)S(1)}, bf16[256,768]{1,0:T(8,128)(2,1)S(1)}, u32[]{:S(2)}, u32[]{:S(2)}) collective-permute-start(bf16[256,768]{1,0:T(8,128)(2,1)S(1)} %get-tuple-element.168.mixed_ref), channel_id=1, source_target_pairs={{0,1},{1,0},{2,3},{3,2},{4,5},{5,4},{6,7},{7,6},{8,9},{9,8},{10,11... | collective-permute-start | bytes 1179656 | tf_op jit(solution)/shard_map/ppermute | solution.py:788
  53.2 15.5 %collective-permute-start.26 = (bf16[2,2,2,96,384]{4,3,2,1,0:T(8,128)(2,1)S(1)}, bf16[2,2,2,96,384]{4,3,2,1,0:T(8,128)(2,1)S(1)}, u32[]{:S(2)}, u32[]{:S(2)}) collective-permute-start(bf16[2,2,2,96,384]{4,3,2,1,0:T(8,128)(2,1)S(1)} %get-tuple-element.165), channel_id=1, source_target_pairs={{0,16},{16,0},{1,17},{17,1},{2,18},{18,2},{3,19},{19,3},{4,20},{20... | collective-permute-start | bytes 1769480 | tf_op jit(solution)/shard_map/ppermute | solution.py:788
  54.8 15.2 %collective-permute-start.27 = (bf16[2,2,2,96,384]{4,3,2,1,0:T(8,128)(2,1)S(1)}, bf16[2,2,2,96,384]{4,3,2,1,0:T(8,128)(2,1)S(1)}, u32[]{:S(2)}, u32[]{:S(2)}) collective-permute-start(bf16[2,2,2,96,384]{4,3,2,1,0:T(8,128)(2,1)S(1)} %get-tuple-element.166), channel_id=1, source_target_pairs={{0,2},{1,3},{2,0},{3,1},{4,6},{5,7},{6,4},{7,5},{8,10},{9,11},{10,... | collective-permute-start | bytes 1769480 | tf_op jit(solution)/shard_map/ppermute | solution.py:788
  84.5 17.3 %collective-permute-start.34 = (bf16[2,192,384]{2,1,0:T(8,128)(2,1)S(1)}, bf16[2,192,384]{2,1,0:T(8,128)(2,1)S(1)}, u32[]{:S(2)}, u32[]{:S(2)}) collective-permute-start(bf16[2,192,384]{2,1,0:T(8,128)(2,1)S(1)} %plane_halves.4), channel_id=1, source_target_pairs={{0,4},{1,5},{2,6},{3,7},{4,0},{5,1},{6,2},{7,3},{8,12},{9,13},{10,... | collective-permute-start | bytes 884744 | tf_op jit(solution)/shard_map/ppermute | solution.py:788
  86.3 18.7 %collective-permute-start.35 = (bf16[2,2,2,48,1024]{4,3,2,1,0:T(8,128)(2,1)S(1)}, bf16[2,2,2,48,1024]{4,3,2,1,0:T(8,128)(2,1)S(1)}, u32[]{:S(2)}, u32[]{:S(2)}) collective-permute-start(bf16[2,2,2,48,1024]{4,3,2,1,0:T(8,128)(2,1)S(1)} %get-tuple-element.206), channel_id=1, source_target_pairs={{0,16},{16,0},{1,17},{17,1},{2,18},{18,2},{3,19},{19,3},{4,20},{20... | collective-permute-start | bytes 2359304 | tf_op jit(solution)/shard_map/ppermute | solution.py:788
  86.8 16.3 %collective-permute-start.36 = (bf16[2,2,2,48,896]{4,3,2,1,0:T(8,128)(2,1)S(1)}, bf16[2,2,2,48,896]{4,3,2,1,0:T(8,128)(2,1)S(1)}, u32[]{:S(2)}, u32[]{:S(2)}) collective-permute-start(bf16[2,2,2,48,896]{4,3,2,1,0:T(8,128)(2,1)S(1)} %get-tuple-element.207), channel_id=1, source_target_pairs={{0,2},{1,3},{2,0},{3,1},{4,6},{5,7},{6,4},{7,5},{8,10},{9,11},{10,... | collective-permute-start | bytes 2064392 | tf_op jit(solution)/shard_map/ppermute | solution.py:788
  87.4 14.3 %collective-permute-start.38 = (bf16[64,768]{1,0:T(8,128)(2,1)S(1)}, bf16[64,768]{1,0:T(8,128)(2,1)S(1)}, u32[]{:S(2)}, u32[]{:S(2)}) collective-permute-start(bf16[64,768]{1,0:T(8,128)(2,1)S(1)} %get-tuple-element.210), channel_id=1, source_target_pairs={{0,8},{1,9},{2,10},{3,11},{4,12},{5,13},{6,14},{7,15},{8,0},{9,1},... | collective-permute-start | bytes 294920 | tf_op jit(solution)/shard_map/ppermute | solution.py:788
  89.2 12.5 %collective-permute-start.39 = (bf16[64,768]{1,0:T(8,128)(2,1)S(1)}, bf16[64,768]{1,0:T(8,128)(2,1)S(1)}, u32[]{:S(2)}, u32[]{:S(2)}) collective-permute-start(bf16[64,768]{1,0:T(8,128)(2,1)S(1)} %get-tuple-element.211), channel_id=1, source_target_pairs={{0,12},{1,13},{2,14},{3,15},{4,8},{5,9},{6,10},{7,11},{8,4},{9,5},... | collective-permute-start | bytes 294920 | tf_op jit(solution)/shard_map/ppermute | solution.py:788
  105.0 18.1 %collective-permute-start.41 = (bf16[9,48,576]{2,1,0:T(8,128)(2,1)S(1)}, bf16[9,48,576]{2,1,0:T(8,128)(2,1)S(1)}, u32[]{:S(2)}, u32[]{:S(2)}) collective-permute-start(bf16[9,48,576]{2,1,0:T(8,128)(2,1)S(1)} %get-tuple-element.219.refs_2_), channel_id=1, source_target_pairs={{0,4},{1,5},{2,6},{3,7},{4,0},{5,1},{6,2},{7,3},{8,12},{9,13},{10,... | collective-permute-start | bytes 1493000 | tf_op jit(solution)/shard_map/ppermute | solution.py:788
  105.5 15.5 %collective-permute-start.43 = (bf16[2,2,48,1024]{3,2,1,0:T(8,128)(2,1)S(1)}, bf16[2,2,48,1024]{3,2,1,0:T(8,128)(2,1)S(1)}, u32[]{:S(2)}, u32[]{:S(2)}) collective-permute-start(bf16[2,2,48,1024]{3,2,1,0:T(8,128)(2,1)S(1)} %get-tuple-element.223), channel_id=1, source_target_pairs={{0,2},{1,3},{2,0},{3,1},{4,6},{5,7},{6,4},{7,5},{8,10},{9,11},{10,... | collective-permute-start | bytes 1179656 | tf_op jit(solution)/shard_map/ppermute | solution.py:788
  107.4 17.9 %collective-permute-start.42 = (bf16[256,768]{1,0:T(8,128)(2,1)S(1)}, bf16[256,768]{1,0:T(8,128)(2,1)S(1)}, u32[]{:S(2)}, u32[]{:S(2)}) collective-permute-start(bf16[256,768]{1,0:T(8,128)(2,1)S(1)} %branch_halves.1), channel_id=1, source_target_pairs={{0,2},{1,3},{2,0},{3,1},{4,6},{5,7},{6,4},{7,5},{8,10},{9,11},{10,... | collective-permute-start | bytes 1179656 | tf_op jit(solution)/shard_map/ppermute | solution.py:788
  107.9 13.0 %collective-permute-start.44 = (bf16[2,2,48,896]{3,2,1,0:T(8,128)(2,1)S(1)}, bf16[2,2,48,896]{3,2,1,0:T(8,128)(2,1)S(1)}, u32[]{:S(2)}, u32[]{:S(2)}) collective-permute-start(bf16[2,2,48,896]{3,2,1,0:T(8,128)(2,1)S(1)} %get-tuple-element.224), channel_id=1, source_target_pairs={{0,16},{16,0},{1,17},{17,1},{2,18},{18,2},{3,19},{19,3},{4,20},{20... | collective-permute-start | bytes 1032200 | tf_op jit(solution)/shard_map/ppermute | solution.py:788
  108.5 12.4 %collective-permute-start.45 = (bf16[192,384]{1,0:T(8,128)(2,1)S(1)}, bf16[192,384]{1,0:T(8,128)(2,1)S(1)}, u32[]{:S(2)}, u32[]{:S(2)}) collective-permute-start(bf16[192,384]{1,0:T(8,128)(2,1)S(1)} %plane_halves.5), channel_id=1, source_target_pairs={{0,8},{1,9},{2,10},{3,11},{4,12},{5,13},{6,14},{7,15},{8,0},{9,1},... | collective-permute-start | bytes 442376 | tf_op jit(solution)/shard_map/ppermute | solution.py:788
  125.3 16.2 %collective-permute-start.49 = (bf16[5,48,576]{2,1,0:T(8,128)(2,1)S(1)}, bf16[5,48,576]{2,1,0:T(8,128)(2,1)S(1)}, u32[]{:S(2)}, u32[]{:S(2)}) collective-permute-start(bf16[5,48,576]{2,1,0:T(8,128)(2,1)S(1)} %joined_halves.1.refs_3_), channel_id=1, source_target_pairs={{0,8},{1,9},{2,10},{3,11},{4,12},{5,13},{6,14},{7,15},{8,0},{9,1},... | collective-permute-start | bytes 829448 | tf_op jit(solution)/shard_map/ppermute | solution.py:788
  127.5 15.3 %collective-permute-start.54 = (bf16[2,48,1920]{2,1,0:T(8,128)(2,1)S(1)}, bf16[2,48,1920]{2,1,0:T(8,128)(2,1)S(1)}, u32[]{:S(2)}, u32[]{:S(2)}) collective-permute-start(bf16[2,48,1920]{2,1,0:T(8,128)(2,1)S(1)} %plane_halves.6), channel_id=1, source_target_pairs={{0,4},{1,5},{2,6},{3,7},{4,0},{5,1},{6,2},{7,3},{8,12},{9,13},{10,... | collective-permute-start | bytes 1105928 | tf_op jit(solution)/shard_map/ppermute | solution.py:788
  142.9 17.3 %collective-permute-start.55 = (bf16[48,1920]{1,0:T(8,128)(2,1)S(1)}, bf16[48,1920]{1,0:T(8,128)(2,1)S(1)}, u32[]{:S(2)}, u32[]{:S(2)}) collective-permute-start(bf16[48,1920]{1,0:T(8,128)(2,1)S(1)} %plane_halves.7), channel_id=1, source_target_pairs={{0,8},{1,9},{2,10},{3,11},{4,12},{5,13},{6,14},{7,15},{8,0},{9,1},... | collective-permute-start | bytes 552968 | tf_op jit(solution)/shard_map/ppermute | solution.py:788
  147.3 12.4 %collective-permute-start.47 = (bf16[64,768]{1,0:T(8,128)(2,1)S(1)}, bf16[64,768]{1,0:T(8,128)(2,1)S(1)}, u32[]{:S(2)}, u32[]{:S(2)}) collective-permute-start(bf16[64,768]{1,0:T(8,128)(2,1)S(1)} %get-tuple-element.229), channel_id=1, source_target_pairs={{0,8},{1,9},{2,10},{3,11},{4,12},{5,13},{6,14},{7,15},{8,0},{9,1},... | collective-permute-start | bytes 294920 | tf_op jit(solution)/shard_map/ppermute | solution.py:788
  147.7 12.6 %collective-permute-start.48 = (bf16[64,768]{1,0:T(8,128)(2,1)S(1)}, bf16[64,768]{1,0:T(8,128)(2,1)S(1)}, u32[]{:S(2)}, u32[]{:S(2)}) collective-permute-start(bf16[64,768]{1,0:T(8,128)(2,1)S(1)} %get-tuple-element.230), channel_id=1, source_target_pairs={{0,12},{1,13},{2,14},{3,15},{4,8},{5,9},{6,10},{7,11},{8,4},{9,5},... | collective-permute-start | bytes 294920 | tf_op jit(solution)/shard_map/ppermute | solution.py:788
  149.9 14.7 %collective-permute-start.57 = (bf16[192,384]{1,0:T(8,128)(2,1)S(1)}, bf16[192,384]{1,0:T(8,128)(2,1)S(1)}, u32[]{:S(2)}, u32[]{:S(2)}) collective-permute-start(bf16[192,384]{1,0:T(8,128)(2,1)S(1)} %last_halves.3.own_ref), channel_id=1, source_target_pairs={{0,16},{16,0},{1,17},{17,1},{2,18},{18,2},{3,19},{19,3},{4,20},{20... | collective-permute-start | bytes 442376 | tf_op jit(solution)/shard_map/ppermute | solution.py:788
  151.5 14.5 %collective-permute-start.51 = (bf16[2,48,576]{2,1,0:T(8,128)(2,1)S(1)}, bf16[2,48,576]{2,1,0:T(8,128)(2,1)S(1)}, u32[]{:S(2)}, u32[]{:S(2)}) collective-permute-start(bf16[2,48,576]{2,1,0:T(8,128)(2,1)S(1)} %get-tuple-element.234), channel_id=1, source_target_pairs={{0,1},{1,0},{2,3},{3,2},{4,5},{5,4},{6,7},{7,6},{8,9},{9,8},{10,11... | collective-permute-start | bytes 331784 | tf_op jit(solution)/shard_map/ppermute | solution.py:788
  (42 other events, 358.0 us)

commit v2 on v1

--- a/solution.py
+++ b/solution.py
@@ -940,10 +940,10 @@
     second_gain = second_gain.reshape(1, width)
     hidden_gain = hidden_gain.reshape(1, spread)
     (
-        first_arrived[-1], place, lengths, gain_row, mixed_gain, second_gain, hidden_gain, own_weight,
+        first_arrived[1], place, lengths, gain_row, mixed_gain, second_gain, hidden_gain, own_weight,
     ) = lax.optimization_barrier(
         (
-            first_arrived[-1], place, lengths, gain_row, mixed_gain, second_gain, hidden_gain,
+            first_arrived[1], place, lengths, gain_row, mixed_gain, second_gain, hidden_gain,
             own_weight,
         )
     )

time: 171 us -> 171 us (level)
  waiting for transfers between devices: 65.1 us -> 62.4 us
  starting transfers between devices: 48.2 us -> 50.3 us
    ppermute x58, waiting for transfers between devices: 65.1 us -> 62.4 us  [swap(): return lax.ppermute(value, axis, [(i, i ^ bits) for i in range(size)])]
    ppermute x58, starting transfers between devices: 48.2 us -> 50.3 us  [swap(): return lax.ppermute(value, axis, [(i, i ^ bits) for i in range(size)])]
  transfers between devices with their start and end apart: 58 -> 58, of which waited for: 26 -> 25; matrix products, arithmetic and copies ran while one was open for 3% -> 3% of each run, Pallas kernels for 23% -> 23%
where the time goes in v2:
time: 171 us; the launch traced here: 170 us
  waiting for transfers between devices  62.4 us (36%)
  starting transfers between devices  50.3 us (29%)
  Pallas kernels  49 us (29%)
  local copies, waits for them, and re-layouts  6.48 us (4%)
    ppermute x58, waiting for transfers between devices, swap(): return lax.ppermute(value, axis, [(i, i ^ bits) for i in range(size)])  62.4 us
    ppermute x58, starting transfers between devices, swap(): return lax.ppermute(value, axis, [(i, i ^ bits) for i in range(size)])  50.3 us
    pallas_call x1, Pallas kernels, backward_call(): pl.pallas_call(kernel, out_shape=(jax.ShapeDtypeStruct((planes * slots //...  11.7 us
    pallas_call x1, Pallas kernels, forward_call(): pl.pallas_call(kernel, out_shape=(pltpu.VMEM((length, width), bf16), pltp...  7.76 us
    pallas_call x1, Pallas kernels, turn_call(): pl.pallas_call(functools.partial(turn_kernel, slots=slots, planes=planes,...  7.09 us
    pallas_call x1, Pallas kernels, widen_call(): pl.pallas_call(functools.partial(widen_kernel, slots=slots, planes=len(in...  7.07 us
    pallas_call x2, Pallas kernels, outer_call(): pl.pallas_call(functools.partial(kernel, cutting=dict(bands=bands, steps=...  5.76 us
  transfers between devices with their start and end apart: 58, of which 25 were waited for; matrix products, arithmetic and copies ran while one was open for 3% of the time, Pallas kernels for 23%

profile of v2, /device:TPU:0, one launch (start us, length us, event | category | flops | bytes accessed | tf_op | source)
XLA Modules:
  0.0 169.6 jit_solution(295344738740739902)
XLA Ops:
  2.3 2.6 %collective-permute-start.2 = (bf16[64,768]{1,0:T(8,128)(2,1)S(1)}, bf16[64,768]{1,0:T(8,128)(2,1)S(1)}, u32[]{:S(2)}, u32[]{:S(2)}) collective-permute-start(bf16[64,768]{1,0:T(8,128)(2,1)S(1)} %get-tuple-element.255.refs_4_.refs_5_.refs_0_), channel_id=1, source_target_pairs={{0,2},{1,3},{2,0},{3,1},{4,6},{5,7},{6,4},{7,5},{8,10},{9,11},{10,... | collective-permute-start | bytes 294920 | tf_op jit(solution)/shard_map/ppermute | solution.py:788
  6.4 2.6 %collective-permute-start.7 = (bf16[64,768]{1,0:T(8,128)(2,1)S(1)}, bf16[64,768]{1,0:T(8,128)(2,1)S(1)}, u32[]{:S(2)}, u32[]{:S(2)}) collective-permute-start(bf16[64,768]{1,0:T(8,128)(2,1)S(1)} %get-tuple-element.257), channel_id=1, source_target_pairs={{0,8},{1,9},{2,10},{3,11},{4,12},{5,13},{6,14},{7,15},{8,0},{9,1},... | collective-permute-start | bytes 294920 | tf_op jit(solution)/shard_map/ppermute | solution.py:788
  11.4 2.0 %constant_dynamic-slice_fusion.2 = (bf16[768,192]{1,0:T(8,128)(2,1)S(1)}, bf16[768,192]{1,0:T(8,128)(2,1)S(1)}, bf16[768,192]{1,0:T(8,128)(2,1)S(1)}) fusion(bf16[768,2304]{1,0:T(8,128)(2,1)} %param.14, s32[]{:T(128)S(6)} %select_n.45, s32[]{:T(128)S(6)} %select_n.47, s32[]{:T(128)S(6)} %select_n.46), kind=kLoop, calls=%fused_computation.14 | loop fusion | bytes 1769484 | tf_op jit(solution)/shard_map/dynamic_slice | solution.py:932
  14.7 2.3 %collective-permute-done.7.refs_12_.refs_7_.refs_2_ = bf16[64,768]{1,0:T(8,128)(2,1)S(1)} collective-permute-done((bf16[64,768]{1,0:T(8,128)(2,1)S(1)}, bf16[64,768]{1,0:T(8,128)(2,1)S(1)}, u32[]{:S(2)}, u32[]{:S(2)}) %collective-permute-start.7) | collective-permute-done | bytes 98336 | tf_op jit(solution)/shard_map/ppermute | solution.py:788
  20.1 2.3 %collective-permute-done.9.refs_14_ = bf16[64,768]{1,0:T(8,128)(2,1)S(1)} collective-permute-done((bf16[64,768]{1,0:T(8,128)(2,1)S(1)}, bf16[64,768]{1,0:T(8,128)(2,1)S(1)}, u32[]{:S(2)}, u32[]{:S(2)}) %collective-permute-start.9) | collective-permute-done | bytes 98336 | tf_op jit(solution)/shard_map/ppermute | solution.py:788
  24.7 7.8 %attention_forward.1 = (bf16[1024,768]{1,0:T(8,128)(2,1)S(1)}, bf16[9,1024,64]{2,1,0:T(8,128)(2,1)S(1)}, f32[1024,3]{1,0:T(8,128)S(1)}, bf16[128,384]{1,0:T(8,12...) custom-call(s32[4]{0:T(128)S(1)} %pad_add_fusion.refs_0_.place_ref, ...), custom_call_target="tpu_custom_call" | custom-call | flops 8589934592 | bytes 8388608 | tf_op jit(solution)/shard_map/attention_forward/pallas_call | solution.py:163
  35.2 3.5 %collective-permute-start.19 = (bf16[64,768]{1,0:T(8,128)(2,1)S(1)}, bf16[64,768]{1,0:T(8,128)(2,1)S(1)}, u32[]{:S(2)}, u32[]{:S(2)}) collective-permute-start(bf16[64,768]{1,0:T(8,128)(2,1)S(1)} %get-tuple-element.251), channel_id=1, source_target_pairs={{0,8},{1,9},{2,10},{3,11},{4,12},{5,13},{6,14},{7,15},{8,0},{9,1},... | collective-permute-start | bytes 294920 | tf_op jit(solution)/shard_map/ppermute | solution.py:788
  39.3 7.1 %widen.1 = (bf16[256,768]{1,0:T(8,128)(2,1)S(1)}, f32[256,768]{1,0:T(8,128)S(1)}, bf16[256,768]{1,0:T(8,128)(2,1)S(1)}, bf16[256,1536]{1,0:T(8,128)(2,1)S(1)}, b...) custom-call(s32[4]{0:T(128)S(1)} %pad_add_fusion.refs_0_.place_ref, ...), custom_call_target="tpu_custom_call" | custom-call | flops 6442450944 | bytes 6291456 | tf_op jit(solution)/shard_map/widen/pallas_call | solution.py:407
  49.5 2.8 %shrink_outer.1 = (bf16[2,2,2,2,192,384]{5,4,3,2,1,0:T(8,128)(2,1)S(1)}, bf16[2,2,2,96,384]{4,3,2,1,0:T(8,128)(2,1)S(1)}, bf16[2,2,2,96,384]{4,3,2,1,0:T(8,128)(2,1)S(1)}) custom-call(s32[4]{0:T(128)S(1)} %pad_add_fusion.refs_0_.place_ref, bf16[256,1536]{1,0:T(8,128)(2,1)S(1)} %get-tuple-element.163.hidden_ref, ...), custom_call_target="tpu_custom_call" | custom-call | flops 2147483648 | bytes 10485760 | tf_op jit(solution)/shard_map/shrink_outer/pallas_call | solution.py:664
  54.4 7.1 %turn.1 = (bf16[256,3072]{1,0:T(8,128)(2,1)S(1)}, bf16[256,768]{1,0:T(8,128)(2,1)S(1)}, f32[256,768]{1,0:T(8,128)S(1)}, f32[1,4608]{1,0:T(1,128)S(1)}, bf16[128,...) custom-call(s32[4]{0:T(128)S(1)} %pad_add_fusion.refs_0_.place_ref, ...), custom_call_target="tpu_custom_call" | custom-call | flops 9663676416 | bytes 8388608 | tf_op jit(solution)/shard_map/turn/pallas_call | solution.py:559
  61.5 6.5 %collective-permute-done.26.refs_1_ = bf16[2,2,2,96,384]{4,3,2,1,0:T(8,128)(2,1)S(1)} collective-permute-done((bf16[2,2,2,96,384]{4,3,2,1,0:T(8,128)(2,1)S(1)}, bf16[2,2,2,96,384]{4,3,2,1,0:T(8,128)(2,1)S(1)}, u32[]{:S(2)}, u32[]{:S(2)}) %collective-permute-start.26) | collective-permute-done | bytes 589856 | tf_op jit(solution)/shard_map/ppermute | solution.py:788
  76.6 3.0 %expand_outer.1 = (bf16[2,2,2,2,48,1920]{5,4,3,2,1,0:T(8,128)(2,1)S(1)}, bf16[2,2,2,48,1024]{4,3,2,1,0:T(8,128)(2,1)S(1)}, bf16[2,2,2,48,896]{4,3,2,1,0:T(8,128)(2,1)S(1)}) custom-call(s32[4]{0:T(128)S(1)} %pad_add_fusion.refs_0_.place_ref, bf16[256,768]{1,0:T(8,128)(2,1)S(1)} %get-tuple-element.167.second_ref, ...), custom_call_target="tpu_custom_call" | custom-call | flops 2147483648 | bytes 10485760 | tf_op jit(solution)/shard_map/expand_outer/pallas_call | solution.py:664
  79.6 1.9 %collective-permute-start.37 = (bf16[64,768]{1,0:T(8,128)(2,1)S(1)}, bf16[64,768]{1,0:T(8,128)(2,1)S(1)}, u32[]{:S(2)}, u32[]{:S(2)}) collective-permute-start(bf16[64,768]{1,0:T(8,128)(2,1)S(1)} %get-tuple-element.209), channel_id=1, source_target_pairs={{0,4},{1,5},{2,6},{3,7},{4,0},{5,1},{6,2},{7,3},{8,12},{9,13},{10,... | collective-permute-start | bytes 294920 | tf_op jit(solution)/shard_map/ppermute | solution.py:788
  83.7 1.9 %collective-permute-start.34 = (bf16[2,192,384]{2,1,0:T(8,128)(2,1)S(1)}, bf16[2,192,384]{2,1,0:T(8,128)(2,1)S(1)}, u32[]{:S(2)}, u32[]{:S(2)}) collective-permute-start(bf16[2,192,384]{2,1,0:T(8,128)(2,1)S(1)} %plane_halves.4), channel_id=1, source_target_pairs={{0,4},{1,5},{2,6},{3,7},{4,0},{5,1},{6,2},{7,3},{8,12},{9,13},{10,... | collective-permute-start | bytes 884744 | tf_op jit(solution)/shard_map/ppermute | solution.py:788
  86.7 2.5 %collective-permute-start.38 = (bf16[64,768]{1,0:T(8,128)(2,1)S(1)}, bf16[64,768]{1,0:T(8,128)(2,1)S(1)}, u32[]{:S(2)}, u32[]{:S(2)}) collective-permute-start(bf16[64,768]{1,0:T(8,128)(2,1)S(1)} %get-tuple-element.210), channel_id=1, source_target_pairs={{0,8},{1,9},{2,10},{3,11},{4,12},{5,13},{6,14},{7,15},{8,0},{9,1},... | collective-permute-start | bytes 294920 | tf_op jit(solution)/shard_map/ppermute | solution.py:788
  89.2 11.7 %attention_backward.1 = (bf16[8,48,576]{2,1,0:T(8,128)(2,1)S(1)}, bf16[9,48,576]{2,1,0:T(8,128)(2,1)S(1)}, bf16[2,256,768]{2,1,0:T(8,128)(2,1)S(1)}, bf16[2,256,768]{2,1,0:T(8,128)(2,1)S(1)}) custom-call(s32[4]{0:T(128)S(1)} %pad_add_fusion.refs_0_.place_ref, bf16[1024,768]{1,0:T(8,128)(2,1)S(1)} %get-tuple-element.132.refs_1_, ...), custom_call_target="tpu_custom_call" | custom-call | flops 10737418240 | bytes 10485760 | tf_op jit(solution)/shard_map/attention_backward/pallas_call | solution.py:286
  107.8 2.6 %collective-permute-start.45 = (bf16[192,384]{1,0:T(8,128)(2,1)S(1)}, bf16[192,384]{1,0:T(8,128)(2,1)S(1)}, u32[]{:S(2)}, u32[]{:S(2)}) collective-permute-start(bf16[192,384]{1,0:T(8,128)(2,1)S(1)} %plane_halves.5), channel_id=1, source_target_pairs={{0,8},{1,9},{2,10},{3,11},{4,12},{5,13},{6,14},{7,15},{8,0},{9,1},... | collective-permute-start | bytes 442376 | tf_op jit(solution)/shard_map/ppermute | solution.py:788
  110.4 9.8 %collective-permute-done.45.refs_4_ = bf16[192,384]{1,0:T(8,128)(2,1)S(1)} collective-permute-done((bf16[192,384]{1,0:T(8,128)(2,1)S(1)}, bf16[192,384]{1,0:T(8,128)(2,1)S(1)}, u32[]{:S(2)}, u32[]{:S(2)}) %collective-permute-start.45) | collective-permute-done | bytes 147488 | tf_op jit(solution)/shard_map/ppermute | solution.py:788
  120.3 2.1 %collective-permute-done.41.refs_1_ = bf16[9,48,576]{2,1,0:T(8,128)(2,1)S(1)} collective-permute-done((bf16[9,48,576]{2,1,0:T(8,128)(2,1)S(1)}, bf16[9,48,576]{2,1,0:T(8,128)(2,1)S(1)}, u32[]{:S(2)}, u32[]{:S(2)}) %collective-permute-start.41) | collective-permute-done | bytes 497696 | tf_op jit(solution)/shard_map/ppermute | solution.py:788
  122.4 2.2 %collective-permute-done.42.refs_8_ = bf16[256,768]{1,0:T(8,128)(2,1)S(1)} collective-permute-done((bf16[256,768]{1,0:T(8,128)(2,1)S(1)}, bf16[256,768]{1,0:T(8,128)(2,1)S(1)}, u32[]{:S(2)}, u32[]{:S(2)}) %collective-permute-start.42) | collective-permute-done | bytes 393248 | tf_op jit(solution)/shard_map/ppermute | solution.py:788
  124.6 2.8 %collective-permute-start.49 = (bf16[5,48,576]{2,1,0:T(8,128)(2,1)S(1)}, bf16[5,48,576]{2,1,0:T(8,128)(2,1)S(1)}, u32[]{:S(2)}, u32[]{:S(2)}) collective-permute-start(bf16[5,48,576]{2,1,0:T(8,128)(2,1)S(1)} %joined_halves.1.refs_3_), channel_id=1, source_target_pairs={{0,8},{1,9},{2,10},{3,11},{4,12},{5,13},{6,14},{7,15},{8,0},{9,1},... | collective-permute-start | bytes 829448 | tf_op jit(solution)/shard_map/ppermute | solution.py:788
  129.1 11.8 %collective-permute-done.49.refs_2_ = bf16[5,48,576]{2,1,0:T(8,128)(2,1)S(1)} collective-permute-done((bf16[5,48,576]{2,1,0:T(8,128)(2,1)S(1)}, bf16[5,48,576]{2,1,0:T(8,128)(2,1)S(1)}, u32[]{:S(2)}, u32[]{:S(2)}) %collective-permute-start.49) | collective-permute-done | bytes 276512 | tf_op jit(solution)/shard_map/ppermute | solution.py:788
  144.6 2.0 %collective-permute-start.46 = (bf16[64,768]{1,0:T(8,128)(2,1)S(1)}, bf16[64,768]{1,0:T(8,128)(2,1)S(1)}, u32[]{:S(2)}, u32[]{:S(2)}) collective-permute-start(bf16[64,768]{1,0:T(8,128)(2,1)S(1)} %get-tuple-element.228), channel_id=1, source_target_pairs={{0,4},{1,5},{2,6},{3,7},{4,0},{5,1},{6,2},{7,3},{8,12},{9,13},{10,... | collective-permute-start | bytes 294920 | tf_op jit(solution)/shard_map/ppermute | solution.py:788
  150.9 8.2 %collective-permute-done.47.refs_2_ = bf16[64,768]{1,0:T(8,128)(2,1)S(1)} collective-permute-done((bf16[64,768]{1,0:T(8,128)(2,1)S(1)}, bf16[64,768]{1,0:T(8,128)(2,1)S(1)}, u32[]{:S(2)}, u32[]{:S(2)}) %collective-permute-start.47) | collective-permute-done | bytes 98336 | tf_op jit(solution)/shard_map/ppermute | solution.py:788
  (145 shorter events, 59.6 us)
Async XLA Ops:
  1.8 12.7 %collective-permute-start.1 = (bf16[64,768]{1,0:T(8,128)(2,1)S(1)}, bf16[64,768]{1,0:T(8,128)(2,1)S(1)}, u32[]{:S(2)}, u32[]{:S(2)}) collective-permute-start(bf16[64,768]{1,0:T(8,128)(2,1)S(1)} %get-tuple-element.255.refs_4_.refs_5_.refs_0_), channel_id=1, source_target_pairs={{0,1},{1,0},{2,3},{3,2},{4,5},{5,4},{6,7},{7,6},{8,9},{9,8},{10,11... | collective-permute-start | bytes 294920 | tf_op jit(solution)/shard_map/ppermute | solution.py:788
  2.3 11.6 %collective-permute-start.2 = (bf16[64,768]{1,0:T(8,128)(2,1)S(1)}, bf16[64,768]{1,0:T(8,128)(2,1)S(1)}, u32[]{:S(2)}, u32[]{:S(2)}) collective-permute-start(bf16[64,768]{1,0:T(8,128)(2,1)S(1)} %get-tuple-element.255.refs_4_.refs_5_.refs_0_), channel_id=1, source_target_pairs={{0,2},{1,3},{2,0},{3,1},{4,6},{5,7},{6,4},{7,5},{8,10},{9,11},{10,... | collective-permute-start | bytes 294920 | tf_op jit(solution)/shard_map/ppermute | solution.py:788
  34.5 11.9 %collective-permute-start.18 = (bf16[64,768]{1,0:T(8,128)(2,1)S(1)}, bf16[64,768]{1,0:T(8,128)(2,1)S(1)}, u32[]{:S(2)}, u32[]{:S(2)}) collective-permute-start(bf16[64,768]{1,0:T(8,128)(2,1)S(1)} %get-tuple-element.252), channel_id=1, source_target_pairs={{0,4},{1,5},{2,6},{3,7},{4,0},{5,1},{6,2},{7,3},{8,12},{9,13},{10,... | collective-permute-start | bytes 294920 | tf_op jit(solution)/shard_map/ppermute | solution.py:788
  47.7 13.7 %collective-permute-start.28 = (bf16[256,768]{1,0:T(8,128)(2,1)S(1)}, bf16[256,768]{1,0:T(8,128)(2,1)S(1)}, u32[]{:S(2)}, u32[]{:S(2)}) collective-permute-start(bf16[256,768]{1,0:T(8,128)(2,1)S(1)} %get-tuple-element.167.second_ref), channel_id=1, source_target_pairs={{0,1},{1,0},{2,3},{3,2},{4,5},{5,4},{6,7},{7,6},{8,9},{9,8},{10,11... | collective-permute-start | bytes 1179656 | tf_op jit(solution)/shard_map/ppermute | solution.py:788
  48.2 13.3 %collective-permute-start.29 = (bf16[256,768]{1,0:T(8,128)(2,1)S(1)}, bf16[256,768]{1,0:T(8,128)(2,1)S(1)}, u32[]{:S(2)}, u32[]{:S(2)}) collective-permute-start(bf16[256,768]{1,0:T(8,128)(2,1)S(1)} %get-tuple-element.168.mixed_ref), channel_id=1, source_target_pairs={{0,1},{1,0},{2,3},{3,2},{4,5},{5,4},{6,7},{7,6},{8,9},{9,8},{10,11... | collective-permute-start | bytes 1179656 | tf_op jit(solution)/shard_map/ppermute | solution.py:788
  52.3 15.7 %collective-permute-start.26 = (bf16[2,2,2,96,384]{4,3,2,1,0:T(8,128)(2,1)S(1)}, bf16[2,2,2,96,384]{4,3,2,1,0:T(8,128)(2,1)S(1)}, u32[]{:S(2)}, u32[]{:S(2)}) collective-permute-start(bf16[2,2,2,96,384]{4,3,2,1,0:T(8,128)(2,1)S(1)} %get-tuple-element.165), channel_id=1, source_target_pairs={{0,16},{16,0},{1,17},{17,1},{2,18},{18,2},{3,19},{19,3},{4,20},{20... | collective-permute-start | bytes 1769480 | tf_op jit(solution)/shard_map/ppermute | solution.py:788
  53.9 15.3 %collective-permute-start.27 = (bf16[2,2,2,96,384]{4,3,2,1,0:T(8,128)(2,1)S(1)}, bf16[2,2,2,96,384]{4,3,2,1,0:T(8,128)(2,1)S(1)}, u32[]{:S(2)}, u32[]{:S(2)}) collective-permute-start(bf16[2,2,2,96,384]{4,3,2,1,0:T(8,128)(2,1)S(1)} %get-tuple-element.166), channel_id=1, source_target_pairs={{0,2},{1,3},{2,0},{3,1},{4,6},{5,7},{6,4},{7,5},{8,10},{9,11},{10,... | collective-permute-start | bytes 1769480 | tf_op jit(solution)/shard_map/ppermute | solution.py:788
  83.7 17.3 %collective-permute-start.34 = (bf16[2,192,384]{2,1,0:T(8,128)(2,1)S(1)}, bf16[2,192,384]{2,1,0:T(8,128)(2,1)S(1)}, u32[]{:S(2)}, u32[]{:S(2)}) collective-permute-start(bf16[2,192,384]{2,1,0:T(8,128)(2,1)S(1)} %plane_halves.4), channel_id=1, source_target_pairs={{0,4},{1,5},{2,6},{3,7},{4,0},{5,1},{6,2},{7,3},{8,12},{9,13},{10,... | collective-permute-start | bytes 884744 | tf_op jit(solution)/shard_map/ppermute | solution.py:788
  85.6 18.7 %collective-permute-start.35 = (bf16[2,2,2,48,1024]{4,3,2,1,0:T(8,128)(2,1)S(1)}, bf16[2,2,2,48,1024]{4,3,2,1,0:T(8,128)(2,1)S(1)}, u32[]{:S(2)}, u32[]{:S(2)}) collective-permute-start(bf16[2,2,2,48,1024]{4,3,2,1,0:T(8,128)(2,1)S(1)} %get-tuple-element.206), channel_id=1, source_target_pairs={{0,16},{16,0},{1,17},{17,1},{2,18},{18,2},{3,19},{19,3},{4,20},{20... | collective-permute-start | bytes 2359304 | tf_op jit(solution)/shard_map/ppermute | solution.py:788
  86.1 16.3 %collective-permute-start.36 = (bf16[2,2,2,48,896]{4,3,2,1,0:T(8,128)(2,1)S(1)}, bf16[2,2,2,48,896]{4,3,2,1,0:T(8,128)(2,1)S(1)}, u32[]{:S(2)}, u32[]{:S(2)}) collective-permute-start(bf16[2,2,2,48,896]{4,3,2,1,0:T(8,128)(2,1)S(1)} %get-tuple-element.207), channel_id=1, source_target_pairs={{0,2},{1,3},{2,0},{3,1},{4,6},{5,7},{6,4},{7,5},{8,10},{9,11},{10,... | collective-permute-start | bytes 2064392 | tf_op jit(solution)/shard_map/ppermute | solution.py:788
  86.7 14.3 %collective-permute-start.38 = (bf16[64,768]{1,0:T(8,128)(2,1)S(1)}, bf16[64,768]{1,0:T(8,128)(2,1)S(1)}, u32[]{:S(2)}, u32[]{:S(2)}) collective-permute-start(bf16[64,768]{1,0:T(8,128)(2,1)S(1)} %get-tuple-element.210), channel_id=1, source_target_pairs={{0,8},{1,9},{2,10},{3,11},{4,12},{5,13},{6,14},{7,15},{8,0},{9,1},... | collective-permute-start | bytes 294920 | tf_op jit(solution)/shard_map/ppermute | solution.py:788
  89.2 11.8 %collective-permute-start.39 = (bf16[64,768]{1,0:T(8,128)(2,1)S(1)}, bf16[64,768]{1,0:T(8,128)(2,1)S(1)}, u32[]{:S(2)}, u32[]{:S(2)}) collective-permute-start(bf16[64,768]{1,0:T(8,128)(2,1)S(1)} %get-tuple-element.211), channel_id=1, source_target_pairs={{0,12},{1,13},{2,14},{3,15},{4,8},{5,9},{6,10},{7,11},{8,4},{9,5},... | collective-permute-start | bytes 294920 | tf_op jit(solution)/shard_map/ppermute | solution.py:788
  104.3 18.1 %collective-permute-start.41 = (bf16[9,48,576]{2,1,0:T(8,128)(2,1)S(1)}, bf16[9,48,576]{2,1,0:T(8,128)(2,1)S(1)}, u32[]{:S(2)}, u32[]{:S(2)}) collective-permute-start(bf16[9,48,576]{2,1,0:T(8,128)(2,1)S(1)} %get-tuple-element.219.refs_2_), channel_id=1, source_target_pairs={{0,4},{1,5},{2,6},{3,7},{4,0},{5,1},{6,2},{7,3},{8,12},{9,13},{10,... | collective-permute-start | bytes 1493000 | tf_op jit(solution)/shard_map/ppermute | solution.py:788
  104.8 15.5 %collective-permute-start.43 = (bf16[2,2,48,1024]{3,2,1,0:T(8,128)(2,1)S(1)}, bf16[2,2,48,1024]{3,2,1,0:T(8,128)(2,1)S(1)}, u32[]{:S(2)}, u32[]{:S(2)}) collective-permute-start(bf16[2,2,48,1024]{3,2,1,0:T(8,128)(2,1)S(1)} %get-tuple-element.223), channel_id=1, source_target_pairs={{0,2},{1,3},{2,0},{3,1},{4,6},{5,7},{6,4},{7,5},{8,10},{9,11},{10,... | collective-permute-start | bytes 1179656 | tf_op jit(solution)/shard_map/ppermute | solution.py:788
  106.6 17.9 %collective-permute-start.42 = (bf16[256,768]{1,0:T(8,128)(2,1)S(1)}, bf16[256,768]{1,0:T(8,128)(2,1)S(1)}, u32[]{:S(2)}, u32[]{:S(2)}) collective-permute-start(bf16[256,768]{1,0:T(8,128)(2,1)S(1)} %branch_halves.1), channel_id=1, source_target_pairs={{0,2},{1,3},{2,0},{3,1},{4,6},{5,7},{6,4},{7,5},{8,10},{9,11},{10,... | collective-permute-start | bytes 1179656 | tf_op jit(solution)/shard_map/ppermute | solution.py:788
  107.2 13.0 %collective-permute-start.44 = (bf16[2,2,48,896]{3,2,1,0:T(8,128)(2,1)S(1)}, bf16[2,2,48,896]{3,2,1,0:T(8,128)(2,1)S(1)}, u32[]{:S(2)}, u32[]{:S(2)}) collective-permute-start(bf16[2,2,48,896]{3,2,1,0:T(8,128)(2,1)S(1)} %get-tuple-element.224), channel_id=1, source_target_pairs={{0,16},{16,0},{1,17},{17,1},{2,18},{18,2},{3,19},{19,3},{4,20},{20... | collective-permute-start | bytes 1032200 | tf_op jit(solution)/shard_map/ppermute | solution.py:788
  107.8 12.4 %collective-permute-start.45 = (bf16[192,384]{1,0:T(8,128)(2,1)S(1)}, bf16[192,384]{1,0:T(8,128)(2,1)S(1)}, u32[]{:S(2)}, u32[]{:S(2)}) collective-permute-start(bf16[192,384]{1,0:T(8,128)(2,1)S(1)} %plane_halves.5), channel_id=1, source_target_pairs={{0,8},{1,9},{2,10},{3,11},{4,12},{5,13},{6,14},{7,15},{8,0},{9,1},... | collective-permute-start | bytes 442376 | tf_op jit(solution)/shard_map/ppermute | solution.py:788
  124.6 16.3 %collective-permute-start.49 = (bf16[5,48,576]{2,1,0:T(8,128)(2,1)S(1)}, bf16[5,48,576]{2,1,0:T(8,128)(2,1)S(1)}, u32[]{:S(2)}, u32[]{:S(2)}) collective-permute-start(bf16[5,48,576]{2,1,0:T(8,128)(2,1)S(1)} %joined_halves.1.refs_3_), channel_id=1, source_target_pairs={{0,8},{1,9},{2,10},{3,11},{4,12},{5,13},{6,14},{7,15},{8,0},{9,1},... | collective-permute-start | bytes 829448 | tf_op jit(solution)/shard_map/ppermute | solution.py:788
  127.5 15.1 %collective-permute-start.54 = (bf16[2,48,1920]{2,1,0:T(8,128)(2,1)S(1)}, bf16[2,48,1920]{2,1,0:T(8,128)(2,1)S(1)}, u32[]{:S(2)}, u32[]{:S(2)}) collective-permute-start(bf16[2,48,1920]{2,1,0:T(8,128)(2,1)S(1)} %plane_halves.6), channel_id=1, source_target_pairs={{0,4},{1,5},{2,6},{3,7},{4,0},{5,1},{6,2},{7,3},{8,12},{9,13},{10,... | collective-permute-start | bytes 1105928 | tf_op jit(solution)/shard_map/ppermute | solution.py:788
  142.7 17.0 %collective-permute-start.55 = (bf16[48,1920]{1,0:T(8,128)(2,1)S(1)}, bf16[48,1920]{1,0:T(8,128)(2,1)S(1)}, u32[]{:S(2)}, u32[]{:S(2)}) collective-permute-start(bf16[48,1920]{1,0:T(8,128)(2,1)S(1)} %plane_halves.7), channel_id=1, source_target_pairs={{0,8},{1,9},{2,10},{3,11},{4,12},{5,13},{6,14},{7,15},{8,0},{9,1},... | collective-permute-start | bytes 552968 | tf_op jit(solution)/shard_map/ppermute | solution.py:788
  146.6 12.5 %collective-permute-start.47 = (bf16[64,768]{1,0:T(8,128)(2,1)S(1)}, bf16[64,768]{1,0:T(8,128)(2,1)S(1)}, u32[]{:S(2)}, u32[]{:S(2)}) collective-permute-start(bf16[64,768]{1,0:T(8,128)(2,1)S(1)} %get-tuple-element.229), channel_id=1, source_target_pairs={{0,8},{1,9},{2,10},{3,11},{4,12},{5,13},{6,14},{7,15},{8,0},{9,1},... | collective-permute-start | bytes 294920 | tf_op jit(solution)/shard_map/ppermute | solution.py:788
  147.7 12.1 %collective-permute-start.48 = (bf16[64,768]{1,0:T(8,128)(2,1)S(1)}, bf16[64,768]{1,0:T(8,128)(2,1)S(1)}, u32[]{:S(2)}, u32[]{:S(2)}) collective-permute-start(bf16[64,768]{1,0:T(8,128)(2,1)S(1)} %get-tuple-element.230), channel_id=1, source_target_pairs={{0,12},{1,13},{2,14},{3,15},{4,8},{5,9},{6,10},{7,11},{8,4},{9,5},... | collective-permute-start | bytes 294920 | tf_op jit(solution)/shard_map/ppermute | solution.py:788
  149.2 14.8 %collective-permute-start.57 = (bf16[192,384]{1,0:T(8,128)(2,1)S(1)}, bf16[192,384]{1,0:T(8,128)(2,1)S(1)}, u32[]{:S(2)}, u32[]{:S(2)}) collective-permute-start(bf16[192,384]{1,0:T(8,128)(2,1)S(1)} %last_halves.3.own_ref), channel_id=1, source_target_pairs={{0,16},{16,0},{1,17},{17,1},{2,18},{18,2},{3,19},{19,3},{4,20},{20... | collective-permute-start | bytes 442376 | tf_op jit(solution)/shard_map/ppermute | solution.py:788
  150.8 14.6 %collective-permute-start.51 = (bf16[2,48,576]{2,1,0:T(8,128)(2,1)S(1)}, bf16[2,48,576]{2,1,0:T(8,128)(2,1)S(1)}, u32[]{:S(2)}, u32[]{:S(2)}) collective-permute-start(bf16[2,48,576]{2,1,0:T(8,128)(2,1)S(1)} %get-tuple-element.234), channel_id=1, source_target_pairs={{0,1},{1,0},{2,3},{3,2},{4,5},{5,4},{6,7},{7,6},{8,9},{9,8},{10,11... | collective-permute-start | bytes 331784 | tf_op jit(solution)/shard_map/ppermute | solution.py:788
  (42 other events, 356.1 us)
